TPU v7x, 128 devices: a whole 4x4x4 slice. The times are simulated.
128 devices in a mesh: row: 32 (over x, y, core), col: 4 (over z).
Axes of the slice: x: 4, y: 4, z: 4, core: 2. Of those that a mesh axis runs over, the one named last changes fastest.
Arguments:
- factor_blocks: bfloat16 [512, 20, 128, 128], P('row', 'col'), may hold values from -0.125 to 0.125
- pattern: int32 [512, 20], P('row', 'col'), may hold values from -1 to 511, as said below
- levels: int32 [512], replicated, may hold values from 0 to 7, as said below
- diag_inverse: float32 [512, 128, 128], P('row')
- right_side: float32 [512, 128, 128], P('row', None, 'col'), may hold values from -6 to 6
Outputs:
- solution: float32 [512, 128, 128], P('row', None, 'col')
Inputs may be any that keep to these rules, and one draw needn't show every extreme that they name: `levels`: each index of row holds 16 consecutive block rows in nondecreasing level order, 1 to 3 of them at every level, 3 at some level. `pattern`: block rows at level 0 have only empty slots; others have between 10 and 20 nonempty slots first, each naming a block row of a lower level.
All inputs are finite; a program needn't handle non-finite values.
Results may differ from a plain program's by a relative error of at most 0.0027.
Values may be sent and summed in bfloat16 or wider, within the bound.
A program may use at most 128 MiB of HBM per device.

v0:
```python
import jax
import jax.numpy as jnp
from jax import lax
from jax.sharding import PartitionSpec as P

LEV = 8
CAP = 3


def extend(array_in, fill_value):
    shape_pad = (CAP,) + array_in.shape[1:]
    return jnp.concatenate([array_in, jnp.full(shape_pad, fill_value, array_in.dtype)], axis=0)


def per_device(factor_blocks, pattern, levels, diag_inverse, right_side):
    row_count = lax.axis_size("row")
    row_index = lax.axis_index("row")
    block_rows = diag_inverse.shape[0]
    block_width = diag_inverse.shape[1]
    rhs_cols = right_side.shape[2]
    table_cols = rhs_cols * lax.axis_size("col")
    level_grid = levels.reshape(row_count, block_rows)
    positions = jnp.arange(block_rows, dtype=jnp.int32)
    earlier = (positions[None, :] < positions[:, None])[None]
    peers_before = (level_grid[:, :, None] == level_grid[:, None, :]) & earlier
    slot_index = jnp.sum(peers_before.astype(jnp.int32), axis=2).reshape(-1)
    owner_row = jnp.arange(levels.shape[0], dtype=jnp.int32) // block_rows
    table_slot = (levels * row_count + owner_row) * CAP + slot_index
    my_levels = lax.dynamic_slice_in_dim(levels, row_index * block_rows, block_rows)
    blocks_all = extend(factor_blocks, 0)
    columns_all = extend(pattern, -1)
    inverse_all = extend(diag_inverse, 0)
    rhs_all = extend(right_side, 0)
    solved_table = jnp.zeros((LEV * row_count * CAP, block_width, table_cols), jnp.bfloat16)
    solution = jnp.zeros((block_rows + CAP, block_width, rhs_cols), jnp.float32)
    for level_now in range(LEV):
        level_start = jnp.sum((my_levels < level_now).astype(jnp.int32))
        level_count = jnp.sum((my_levels == level_now).astype(jnp.int32))
        blocks_now = lax.dynamic_slice_in_dim(blocks_all, level_start, CAP, 0)
        columns = lax.dynamic_slice_in_dim(columns_all, level_start, CAP, 0)
        inverse_now = lax.dynamic_slice_in_dim(inverse_all, level_start, CAP, 0)
        rhs_now = lax.dynamic_slice_in_dim(rhs_all, level_start, CAP, 0)
        present = columns >= 0
        lookup = table_slot[jnp.where(present, columns, 0)]
        pieces = solved_table[lookup] * present[:, :, None, None].astype(jnp.bfloat16)
        partial_sum = jnp.einsum(
            "ckab,ckbr->car", blocks_now, pieces, preferred_element_type=jnp.float32
        )
        partial_sum = lax.psum_scatter(partial_sum, "col", scatter_dimension=2, tiled=True)
        solved = jnp.einsum(
            "cab,cbr->car", inverse_now, rhs_now - partial_sum, precision=lax.Precision.HIGHEST
        )
        filled = jnp.arange(CAP, dtype=jnp.int32) < level_count
        solved = jnp.where(filled[:, None, None], solved, 0.0)
        solution = lax.dynamic_update_slice_in_dim(solution, solved, level_start, 0)
        if level_now + 1 < LEV:
            solved_bf16 = solved.astype(jnp.bfloat16)
            solved_bf16 = lax.all_gather(solved_bf16, "col", axis=2, tiled=True)
            gathered = lax.all_gather(solved_bf16, "row", axis=0, tiled=True)
            solved_table = lax.dynamic_update_slice_in_dim(
                solved_table, gathered, level_now * row_count * CAP, 0
            )
    return solution[:block_rows]


def solution(mesh):
    return jax.shard_map(
        per_device,
        mesh=mesh,
        in_specs=(
            P("row", "col", None, None),
            P("row", "col"),
            P(),
            P("row", None, None),
            P("row", None, "col"),
        ),
        out_specs=P("row", None, "col"),
        check_vma=False,
    )
```

profile of v0, /device:TPU:1, one launch (start us, length us, event | category | flops | bytes accessed | tf_op | source)
XLA Modules:
  0.0 758.4 jit_solution(15809289860259340521)
XLA Ops:
  6.5 1.7 fusion.69
  23.7 1.1 compare_convert_fusion
  24.8 1.1 compare_select_fusion
  29.0 8.9 %broadcast_in_dim.125 = bf16[768,128,128]{2,1,0:T(8,128)(2,1)} broadcast(bf16[]{:T(256)} %constant.32.clone.1), dimensions={} | broadcast | bytes 25165826 | tf_op jit(solution)/shard_map/broadcast_in_dim | solution.py:34
  37.9 8.8 %gather_fusion.1 = bf16[15,128,128]{2,1,0:T(8,128)(2,1)S(1)} fusion(bf16[768,128,128]{2,1,0:T(8,128)(2,1)} %broadcast_in_dim.125, s32[1024]{0:T(1024)S(1)} %pad_clamp_fusion.14), kind=kCustom, calls=%fused_computation.1 | custom fusion | bytes 983100 | tf_op jit(solution)/shard_map/gather | solution.py:45
  47.7 2.1 convolution_bitcast_fusion.7
  50.5 21.2 %reduce-scatter.9.cloned.1.call-done = f32[3,128,32]{1,2,0:T(8,128)} async-done(((f32[3,128,128]{1,2,0:T(8,128)}), f32[3,128,32]{1,2,0:T(8,128)}) %reduce-scatter.9.cloned.1.call-update) | async-done | bytes 49168 | tf_op jit(solution)/shard_map/reduce_scatter | solution.py:49
  72.4 2.0 fusion.93
  74.4 9.0 %all_gather.42 = bf16[3,128,128]{1,2,0:T(8,128)(2,1)S(1)} all-gather(bf16[3,128,32]{1,2,0:T(8,128)(2,1)S(1)} %get-tuple-element.33), channel_id=1, replica_groups=mesh['row'=32,'col'=4] {'col'}, dimensions={2}, use_global_device_ids=true | all-gather | bytes 122880 | tf_op jit(solution)/shard_map/all_gather | solution.py:58
  84.5 50.0 %all-gather.8.cloned.1.call-done = bf16[96,128,128]{2,1,0:T(8,128)(2,1)} async-done(((bf16[3,128,128]{2,1,0:T(8,128)(2,1)}), bf16[96,128,128]{2,1,0:T(8,128)(2,1)}) %all-gather.8.cloned.1.call-update) | async-done | bytes 3145744 | tf_op jit(solution)/shard_map/all_gather | solution.py:59
  134.5 10.3 %dynamic_update_slice.46 = bf16[768,128,128]{2,1,0:T(8,128)(2,1)} pad(bf16[96,128,128]{2,1,0:T(8,128)(2,1)} %all-gather.8.cloned.1.call-done, bf16[]{:T(256)} %constant.32.clone.1), padding=0_672x0_0x0_0 | pad | bytes 28311554 | tf_op jit(solution)/shard_map/dynamic_update_slice | solution.py:60
  144.8 9.6 %gather_fusion.3 = bf16[15,128,128]{2,1,0:T(8,128)(2,1)} fusion(bf16[768,128,128]{2,1,0:T(8,128)(2,1)} %dynamic_update_slice.46, s32[1024]{0:T(1024)S(1)} %pad_clamp_fusion.12), kind=kCustom, calls=%fused_computation.3 | custom fusion | bytes 983100 | tf_op jit(solution)/shard_map/gather | solution.py:45
  154.4 1.3 copy.108
  155.7 1.0 convolution_bitcast_fusion.6
  157.5 16.9 %reduce-scatter.11.cloned.1.call-done = f32[3,128,32]{1,2,0:T(8,128)} async-done(((f32[3,128,128]{1,2,0:T(8,128)}), f32[3,128,32]{1,2,0:T(8,128)}) %reduce-scatter.11.cloned.1.call-update) | async-done | bytes 49168 | tf_op jit(solution)/shard_map/reduce_scatter | solution.py:49
  174.4 2.0 fusion.92
  176.4 9.0 %all_gather.44 = bf16[3,128,128]{1,2,0:T(8,128)(2,1)S(1)} all-gather(bf16[3,128,32]{1,2,0:T(8,128)(2,1)S(1)} %get-tuple-element.31), channel_id=1, replica_groups=mesh['row'=32,'col'=4] {'col'}, dimensions={2}, use_global_device_ids=true | all-gather | bytes 122880 | tf_op jit(solution)/shard_map/all_gather | solution.py:58
  188.4 48.1 %all-gather.10.cloned.1.call-done = bf16[96,128,128]{2,1,0:T(8,128)(2,1)} async-done(((bf16[3,128,128]{2,1,0:T(8,128)(2,1)}), bf16[96,128,128]{2,1,0:T(8,128)(2,1)}) %all-gather.10.cloned.1.call-update) | async-done | bytes 3145744 | tf_op jit(solution)/shard_map/all_gather | solution.py:59
  236.5 4.0 constant_dynamic-update-slice_fusion.9
  240.5 9.6 %gather_fusion.5 = bf16[15,128,128]{2,1,0:T(8,128)(2,1)} fusion(bf16[768,128,128]{2,1,0:T(8,128)(2,1)} %constant_dynamic-update-slice_fusion.9, s32[1024]{0:T(1024)S(1)} %pad_clamp_fusion.10), kind=kCustom, calls=%fused_computation.5 | custom fusion | bytes 983100 | tf_op jit(solution)/shard_map/gather | solution.py:45
  250.1 1.3 copy.112
  251.4 1.1 convolution_bitcast_fusion.5
  253.2 17.0 %reduce-scatter.13.cloned.1.call-done = f32[3,128,32]{1,2,0:T(8,128)} async-done(((f32[3,128,128]{1,2,0:T(8,128)}), f32[3,128,32]{1,2,0:T(8,128)}) %reduce-scatter.13.cloned.1.call-update) | async-done | bytes 49168 | tf_op jit(solution)/shard_map/reduce_scatter | solution.py:49
  270.1 2.0 fusion.91
  272.1 9.0 %all_gather.46 = bf16[3,128,128]{1,2,0:T(8,128)(2,1)S(1)} all-gather(bf16[3,128,32]{1,2,0:T(8,128)(2,1)S(1)} %get-tuple-element.29), channel_id=1, replica_groups=mesh['row'=32,'col'=4] {'col'}, dimensions={2}, use_global_device_ids=true | all-gather | bytes 122880 | tf_op jit(solution)/shard_map/all_gather | solution.py:58
  282.2 50.0 %all-gather.12.cloned.1.call-done = bf16[96,128,128]{2,1,0:T(8,128)(2,1)} async-done(((bf16[3,128,128]{2,1,0:T(8,128)(2,1)}), bf16[96,128,128]{2,1,0:T(8,128)(2,1)}) %all-gather.12.cloned.1.call-update) | async-done | bytes 3145744 | tf_op jit(solution)/shard_map/all_gather | solution.py:59
  332.1 4.0 constant_dynamic-update-slice_fusion.7
  336.2 9.6 %gather_fusion.7 = bf16[15,128,128]{2,1,0:T(8,128)(2,1)} fusion(bf16[768,128,128]{2,1,0:T(8,128)(2,1)} %constant_dynamic-update-slice_fusion.7, s32[1024]{0:T(1024)S(1)} %pad_clamp_fusion.8), kind=kCustom, calls=%fused_computation.7 | custom fusion | bytes 983100 | tf_op jit(solution)/shard_map/gather | solution.py:45
  345.8 1.3 copy.116
  347.1 1.1 convolution_bitcast_fusion.4
  348.8 16.9 %reduce-scatter.15.cloned.1.call-done = f32[3,128,32]{1,2,0:T(8,128)} async-done(((f32[3,128,128]{1,2,0:T(8,128)}), f32[3,128,32]{1,2,0:T(8,128)}) %reduce-scatter.15.cloned.1.call-update) | async-done | bytes 49168 | tf_op jit(solution)/shard_map/reduce_scatter | solution.py:49
  365.8 2.0 fusion.90
  367.7 9.0 %all_gather.48 = bf16[3,128,128]{1,2,0:T(8,128)(2,1)S(1)} all-gather(bf16[3,128,32]{1,2,0:T(8,128)(2,1)S(1)} %get-tuple-element.27), channel_id=1, replica_groups=mesh['row'=32,'col'=4] {'col'}, dimensions={2}, use_global_device_ids=true | all-gather | bytes 122880 | tf_op jit(solution)/shard_map/all_gather | solution.py:58
  379.7 48.1 %all-gather.14.cloned.1.call-done = bf16[96,128,128]{2,1,0:T(8,128)(2,1)} async-done(((bf16[3,128,128]{2,1,0:T(8,128)(2,1)}), bf16[96,128,128]{2,1,0:T(8,128)(2,1)}) %all-gather.14.cloned.1.call-update) | async-done | bytes 3145744 | tf_op jit(solution)/shard_map/all_gather | solution.py:59
  427.8 3.9 constant_dynamic-update-slice_fusion.5
  431.7 9.6 %gather_fusion.9 = bf16[15,128,128]{2,1,0:T(8,128)(2,1)} fusion(bf16[768,128,128]{2,1,0:T(8,128)(2,1)} %constant_dynamic-update-slice_fusion.5, s32[1024]{0:T(1024)S(1)} %pad_clamp_fusion.6), kind=kCustom, calls=%fused_computation.9 | custom fusion | bytes 983100 | tf_op jit(solution)/shard_map/gather | solution.py:45
  441.4 1.3 copy.120
  442.7 1.0 convolution_bitcast_fusion.3
  444.3 17.0 %reduce-scatter.17.cloned.1.call-done = f32[3,128,32]{1,2,0:T(8,128)} async-done(((f32[3,128,128]{1,2,0:T(8,128)}), f32[3,128,32]{1,2,0:T(8,128)}) %reduce-scatter.17.cloned.1.call-update) | async-done | bytes 49168 | tf_op jit(solution)/shard_map/reduce_scatter | solution.py:49
  461.4 2.0 fusion.89
  463.3 9.0 %all_gather.50 = bf16[3,128,128]{1,2,0:T(8,128)(2,1)S(1)} all-gather(bf16[3,128,32]{1,2,0:T(8,128)(2,1)S(1)} %get-tuple-element.25), channel_id=1, replica_groups=mesh['row'=32,'col'=4] {'col'}, dimensions={2}, use_global_device_ids=true | all-gather | bytes 122880 | tf_op jit(solution)/shard_map/all_gather | solution.py:58
  473.4 50.0 %all-gather.16.cloned.1.call-done = bf16[96,128,128]{2,1,0:T(8,128)(2,1)} async-done(((bf16[3,128,128]{2,1,0:T(8,128)(2,1)}), bf16[96,128,128]{2,1,0:T(8,128)(2,1)}) %all-gather.16.cloned.1.call-update) | async-done | bytes 3145744 | tf_op jit(solution)/shard_map/all_gather | solution.py:59
  523.4 4.0 constant_dynamic-update-slice_fusion.3
  527.4 9.6 %gather_fusion.11 = bf16[15,128,128]{2,1,0:T(8,128)(2,1)} fusion(bf16[768,128,128]{2,1,0:T(8,128)(2,1)} %constant_dynamic-update-slice_fusion.3, s32[1024]{0:T(1024)S(1)} %pad_clamp_fusion.4), kind=kCustom, calls=%fused_computation.11 | custom fusion | bytes 983100 | tf_op jit(solution)/shard_map/gather | solution.py:45
  537.0 1.3 copy.124
  538.3 1.0 convolution_bitcast_fusion.2
  540.1 16.9 %reduce-scatter.19.cloned.1.call-done = f32[3,128,32]{1,2,0:T(8,128)} async-done(((f32[3,128,128]{1,2,0:T(8,128)}), f32[3,128,32]{1,2,0:T(8,128)}) %reduce-scatter.19.cloned.1.call-update) | async-done | bytes 49168 | tf_op jit(solution)/shard_map/reduce_scatter | solution.py:49
  557.0 2.0 fusion.88
  559.0 9.0 %all_gather.52 = bf16[3,128,128]{1,2,0:T(8,128)(2,1)S(1)} all-gather(bf16[3,128,32]{1,2,0:T(8,128)(2,1)S(1)} %get-tuple-element.23), channel_id=1, replica_groups=mesh['row'=32,'col'=4] {'col'}, dimensions={2}, use_global_device_ids=true | all-gather | bytes 122880 | tf_op jit(solution)/shard_map/all_gather | solution.py:58
  570.9 48.1 %all-gather.18.cloned.1.call-done = bf16[96,128,128]{2,1,0:T(8,128)(2,1)} async-done(((bf16[3,128,128]{2,1,0:T(8,128)(2,1)}), bf16[96,128,128]{2,1,0:T(8,128)(2,1)}) %all-gather.18.cloned.1.call-update) | async-done | bytes 3145744 | tf_op jit(solution)/shard_map/all_gather | solution.py:59
  619.0 4.0 constant_dynamic-update-slice_fusion.1
  623.0 9.6 %gather_fusion.13 = bf16[15,128,128]{2,1,0:T(8,128)(2,1)} fusion(bf16[768,128,128]{2,1,0:T(8,128)(2,1)} %constant_dynamic-update-slice_fusion.1, s32[1024]{0:T(1024)S(1)} %pad_clamp_fusion.2), kind=kCustom, calls=%fused_computation.13 | custom fusion | bytes 983100 | tf_op jit(solution)/shard_map/gather | solution.py:45
  632.6 1.3 copy.128
  633.9 1.0 convolution_bitcast_fusion.1
  635.6 17.0 %reduce-scatter.21.cloned.1.call-done = f32[3,128,32]{1,2,0:T(8,128)} async-done(((f32[3,128,128]{1,2,0:T(8,128)}), f32[3,128,32]{1,2,0:T(8,128)}) %reduce-scatter.21.cloned.1.call-update) | async-done | bytes 49168 | tf_op jit(solution)/shard_map/reduce_scatter | solution.py:49
  652.6 2.0 fusion.87
  654.6 9.0 %all_gather.54 = bf16[3,128,128]{1,2,0:T(8,128)(2,1)S(1)} all-gather(bf16[3,128,32]{1,2,0:T(8,128)(2,1)S(1)} %get-tuple-element.21), channel_id=1, replica_groups=mesh['row'=32,'col'=4] {'col'}, dimensions={2}, use_global_device_ids=true | all-gather | bytes 122880 | tf_op jit(solution)/shard_map/all_gather | solution.py:58
  664.7 50.0 %all-gather.20.cloned.1.call-done = bf16[96,128,128]{2,1,0:T(8,128)(2,1)} async-done(((bf16[3,128,128]{2,1,0:T(8,128)(2,1)}), bf16[96,128,128]{2,1,0:T(8,128)(2,1)}) %all-gather.20.cloned.1.call-update) | async-done | bytes 3145744 | tf_op jit(solution)/shard_map/all_gather | solution.py:59
  714.7 4.0 constant_dynamic-update-slice_fusion.11
  718.6 8.8 %gather_fusion.15 = bf16[15,128,128]{2,1,0:T(8,128)(2,1)S(1)} fusion(bf16[768,128,128]{2,1,0:T(8,128)(2,1)} %constant_dynamic-update-slice_fusion.11, s32[1024]{0:T(1024)S(1)} %pad_clamp_fusion), kind=kCustom, calls=%fused_computation.15 | custom fusion | bytes 983100 | tf_op jit(solution)/shard_map/gather | solution.py:45
  728.5 2.1 convolution_bitcast_fusion
  731.2 17.0 %reduce-scatter.23.cloned.1.call-done = f32[3,128,32]{1,2,0:T(8,128)} async-done(((f32[3,128,128]{1,2,0:T(8,128)}), f32[3,128,32]{1,2,0:T(8,128)}) %reduce-scatter.23.cloned.1.call-update) | async-done | bytes 49168 | tf_op jit(solution)/shard_map/reduce_scatter | solution.py:49
  748.2 2.0 fusion
  750.2 1.7 slice.36
  (127 shorter events, 24.7 us)
Async XLA Ops:
  6.5 65.1 %reduce-scatter.9.cloned.1.call-start = ((), (), s32[]{:S(2)}) async-start(), calls=%async_computation.8 | async-start | bytes 245760 | tf_op jit(solution)/shard_map/reduce_scatter | solution.py:49
  29.0 18.7 %copy-start = (bf16[16,5,128,128]{3,2,1,0:T(8,128)(2,1)S(1)}, bf16[16,5,128,128]{3,2,1,0:T(8,128)(2,1)}, u32[]{:S(2)}) copy-start(bf16[16,5,128,128]{3,2,1,0:T(8,128)(2,1)} %param.5) | copy-start | bytes 7864324
  37.9 34.6 %copy-start.1 = (f32[16,128,32]{1,2,0:T(8,128)S(1)}, f32[16,128,32]{1,2,0:T(8,128)}, u32[]{:S(2)}) copy-start(f32[16,128,32]{1,2,0:T(8,128)} %param.9) | copy-start | bytes 786436
  49.8 84.7 %all-gather.8.cloned.1.call-start = ((), (), s32[]{:S(2)}) async-start(), calls=%async_computation.9 | async-start | bytes 3244032 | tf_op jit(solution)/shard_map/all_gather | solution.py:59
  84.2 90.2 %reduce-scatter.11.cloned.1.call-start = ((), (), s32[]{:S(2)}) async-start(), calls=%async_computation.10 | async-start | bytes 245760 | tf_op jit(solution)/shard_map/reduce_scatter | solution.py:49
  156.8 79.7 %all-gather.10.cloned.1.call-start = ((), (), s32[]{:S(2)}) async-start(), calls=%async_computation.11 | async-start | bytes 3244032 | tf_op jit(solution)/shard_map/all_gather | solution.py:59
  186.2 83.9 %reduce-scatter.13.cloned.1.call-start = ((), (), s32[]{:S(2)}) async-start(), calls=%async_computation.12 | async-start | bytes 245760 | tf_op jit(solution)/shard_map/reduce_scatter | solution.py:49
  252.5 79.7 %all-gather.12.cloned.1.call-start = ((), (), s32[]{:S(2)}) async-start(), calls=%async_computation.13 | async-start | bytes 3244032 | tf_op jit(solution)/shard_map/all_gather | solution.py:59
  281.9 83.9 %reduce-scatter.15.cloned.1.call-start = ((), (), s32[]{:S(2)}) async-start(), calls=%async_computation.14 | async-start | bytes 245760 | tf_op jit(solution)/shard_map/reduce_scatter | solution.py:49
  348.1 79.7 %all-gather.14.cloned.1.call-start = ((), (), s32[]{:S(2)}) async-start(), calls=%async_computation.15 | async-start | bytes 3244032 | tf_op jit(solution)/shard_map/all_gather | solution.py:59
  377.6 83.8 %reduce-scatter.17.cloned.1.call-start = ((), (), s32[]{:S(2)}) async-start(), calls=%async_computation.16 | async-start | bytes 245760 | tf_op jit(solution)/shard_map/reduce_scatter | solution.py:49
  443.7 79.7 %all-gather.16.cloned.1.call-start = ((), (), s32[]{:S(2)}) async-start(), calls=%async_computation.17 | async-start | bytes 3244032 | tf_op jit(solution)/shard_map/all_gather | solution.py:59
  473.2 83.8 %reduce-scatter.19.cloned.1.call-start = ((), (), s32[]{:S(2)}) async-start(), calls=%async_computation.18 | async-start | bytes 245760 | tf_op jit(solution)/shard_map/reduce_scatter | solution.py:49
  539.4 79.7 %all-gather.18.cloned.1.call-start = ((), (), s32[]{:S(2)}) async-start(), calls=%async_computation.19 | async-start | bytes 3244032 | tf_op jit(solution)/shard_map/all_gather | solution.py:59
  568.8 83.9 %reduce-scatter.21.cloned.1.call-start = ((), (), s32[]{:S(2)}) async-start(), calls=%async_computation.20 | async-start | bytes 245760 | tf_op jit(solution)/shard_map/reduce_scatter | solution.py:49
  635.0 79.7 %all-gather.20.cloned.1.call-start = ((), (), s32[]{:S(2)}) async-start(), calls=%async_computation.21 | async-start | bytes 3244032 | tf_op jit(solution)/shard_map/all_gather | solution.py:59
  664.4 83.8 %reduce-scatter.23.cloned.1.call-start = ((), (), s32[]{:S(2)}) async-start(), calls=%async_computation.22 | async-start | bytes 245760 | tf_op jit(solution)/shard_map/reduce_scatter | solution.py:49
Sparse Core Ops, SparseCore 0:
  49.9 21.7 reduce-scatter.8
  84.3 50.0 all-gather.7
  156.9 17.4 reduce-scatter.10
  186.3 50.0 all-gather.9
  252.6 17.4 reduce-scatter.12
  282.0 50.0 all-gather.11
  348.3 17.4 reduce-scatter.14
  377.7 50.0 all-gather.13
  443.8 17.4 reduce-scatter.16
  473.3 50.0 all-gather.15
  539.5 17.4 reduce-scatter.18
  568.9 50.0 all-gather.17
  635.1 17.4 reduce-scatter.20
  664.5 50.0 all-gather.19
  730.7 17.4 reduce-scatter.22
where the time goes:
time: 762 us; the launch traced here: 758 us
  waiting for transfers between devices  485 us (64%)
  local copies, waits for them, and re-layouts  146 us (19%)
  blocking collectives  63.2 us (8%)
  between operations  28.2 us (4%)
  matrix products  26.2 us (3%)
  other arithmetic  9.78 us (1%)
    all_gather x7, waiting for transfers between devices, per_device(): gathered = lax.all_gather(solved_bf16, 'row', axis=0, tiled=True)  344 us
    reduce_scatter x8, waiting for transfers between devices, per_device(): lax.psum_scatter(partial_sum, 'col', scatter_dimension=2, tiled=True)  140 us
    gather x16, local copies, waits for them, and re-layouts, per_device(): solved_table[lookup] * present[:, :, None, None].astype(jnp.bfloat16)  85.1 us
    all_gather x7, blocking collectives, per_device(): solved_bf16 = lax.all_gather(solved_bf16, 'col', axis=2, tiled=True)  63.2 us
    dynamic_update_slice x7, local copies, waits for them, and re-layouts, per_device(): lax.dynamic_update_slice_in_dim(solved_table, gathered, level_now * row_c...  34.2 us
    dot_general x8, matrix products, per_device(): jnp.einsum('cab,cbr->car', inverse_now, rhs_now - partial_sum, precision=...  15.8 us
  transfers between devices with their start and end apart: 15, of which 15 were waited for; matrix products, arithmetic and copies ran while one was open for 2% of the time, Pallas kernels for 0%

commit v1 on v0

v1 whole, which is shorter than its diff:
```python
import jax
import jax.numpy as jnp
from jax import lax
from jax.experimental import pallas as pl
from jax.experimental.pallas import tpu as pltpu
from jax.sharding import PartitionSpec as P

MESH = pl.DeviceIdType.MESH
LEV = 8
CAP = 3
B = 128
W = 16
ROWS = 16
SLOTS = 5
EMPTY = (LEV - 1) * CAP * 32
ORDERS = ((0, 1, 2), (1, 2, 0), (2, 0, 1))


def dot_t(a, b):
    return lax.dot_general(a, b, (((1,), (1,)), ((), ())), preferred_element_type=jnp.float32)


def split(a):
    high = a.astype(jnp.bfloat16)
    return high, (a - high.astype(jnp.float32)).astype(jnp.bfloat16)


def times_inverse(v, d):
    n = v.shape[0]
    v_high, v_low = split(v)
    d_high, d_low = split(d)
    both = dot_t(jnp.concatenate([v_high, v_low], axis=0), d_high)
    return both[:n] + (both[n:] + dot_t(v_high, d_low))


def kernel(
    factor, pattern, levels, inverse, rhs, out,
    blocks, inv0, inv, rhs_other, pat_other, table, land, sums, sums_in, x0, x0_in, sol, sol_other, lookup, rows,
    local_sem, start_s, start_r, p0s, p0r, p1s, p1r, p2s, p2r, red_s, red_r, sol_s, sol_r,
):
    row, z = lax.axis_index("row"), lax.axis_index("col")
    x, y, q = row // 8, lax.rem(row // 2, 4), lax.rem(row, 2)
    me = (x, y, z)
    other = 1 - q

    def device(xyz, core):
        return ((xyz[0] * 4 + xyz[1]) * 2 + core, xyz[2])

    def moved(dim, by):
        xyz = list(me)
        xyz[dim] = lax.rem(me[dim] + by, 4)
        return device(xyz, q)

    partner = device(me, other)

    def remote(src, dst, s, r, to):
        return pltpu.make_async_remote_copy(
            src_ref=src, dst_ref=dst, send_sem=s, recv_sem=r, device_id=to, device_id_type=MESH
        )

    own = [
        pltpu.make_async_copy(inverse.at[0:CAP], inv0, local_sem.at[0]),
        pltpu.make_async_copy(inverse, inv.at[0], local_sem.at[1]),
        pltpu.make_async_copy(factor, blocks.at[0], local_sem.at[2]),
    ]
    for c in own:
        c.start()

    barrier = pltpu.get_barrier_semaphore()
    greeted = [partner] + [moved(d, by) for d in range(3) for by in (1, 2, 3)]
    for to in greeted:
        pl.semaphore_signal(barrier, inc=1, device_id=to, device_id_type=MESH)
    table[EMPTY] = jnp.zeros(table.shape[1:], table.dtype)
    pl.semaphore_wait(barrier, len(greeted))

    def start_copies():
        return [
            remote(pattern, pat_other, start_s.at[0], start_r.at[0], partner),
            remote(rhs.at[:, other], rhs_other, start_s.at[1], start_r.at[1], partner),
            remote(inverse, inv.at[1], start_s.at[2], start_r.at[2], partner),
            remote(factor, blocks.at[1], start_s.at[3], start_r.at[3], partner),
        ]

    x0_copy = remote(x0.at[other], x0_in, start_s.at[4], start_r.at[4], partner)

    def place(c):
        d0, d1, d2 = ORDERS[c]
        return me[d2] * 16 + me[d1] * 4 + me[d0]

    own[0].wait()
    for c in range(CAP):
        v = times_inverse(rhs[c].reshape(2 * W, B), inv0[c]).reshape(2, W, B)
        sol[:, c] = v
        x0[:, c] = v.astype(jnp.bfloat16)
    x0_copy.start()
    for copy in start_copies():
        copy.start()
    for c in range(CAP):
        land[0, c, place(c), q] = x0[q, c]
    x0_copy.wait()
    for c in range(CAP):
        land[0, c, place(c), other] = x0_in[c]

    def phase0(p, c):
        d0 = ORDERS[c][0]
        unit = land.at[p, c, pl.ds(place(c), 1)]
        return [
            remote(unit, unit, p0s.at[p, 3 * c + by - 1], p0r.at[p, 3 * c + by - 1], moved(d0, by)) for by in (1, 2, 3)
        ]

    def phase0_in(p, c):
        d0, d1, d2 = ORDERS[c]
        result = []
        for by in (1, 2, 3):
            at = me[d2] * 16 + me[d1] * 4 + lax.rem(me[d0] + 4 - by, 4)
            unit = land.at[p, c, pl.ds(at, 1)]
            result.append(remote(unit, unit, p0s.at[p, 3 * c + by - 1], p0r.at[p, 3 * c + by - 1], moved(d0, by)))
        return result

    def phase1(p, c):
        d0, d1, d2 = ORDERS[c]
        unit = land.at[p, c, pl.ds(me[d2] * 16 + me[d1] * 4, 4)]
        return [
            remote(unit, unit, p1s.at[p, 3 * c + by - 1], p1r.at[p, 3 * c + by - 1], moved(d1, by)) for by in (1, 2, 3)
        ]

    def phase1_in(p, c):
        d0, d1, d2 = ORDERS[c]
        result = []
        for by in (1, 2, 3):
            unit = land.at[p, c, pl.ds(me[d2] * 16 + lax.rem(me[d1] + 4 - by, 4) * 4, 4)]
            result.append(remote(unit, unit, p1s.at[p, 3 * c + by - 1], p1r.at[p, 3 * c + by - 1], moved(d1, by)))
        return result

    RING = ((0, 0, 1), (0, 1, 1), (0, 1, 3), (0, 0, 3), (3, 0, 1), (1, 1, 3))

    def phase2(p, c, k):
        d2 = ORDERS[c][2]
        owner, half, to = RING[k]
        unit = land.at[p, c, pl.ds(lax.rem(me[d2] + owner, 4) * 16 + half * 8, 8)]
        return remote(unit, unit, p2s.at[p, 6 * c + k], p2r.at[p, 6 * c + k], moved(d2, to))

    def phase2_in(p, c, k):
        d2 = ORDERS[c][2]
        owner, half, to = RING[k]
        unit = land.at[p, c, pl.ds(lax.rem(me[d2] + owner + 4 - to, 4) * 16 + half * 8, 8)]
        return remote(unit, unit, p2s.at[p, 6 * c + k], p2r.at[p, 6 * c + k], moved(d2, to))

    def sums_copy(p, by):
        to = lax.rem(z + by, 4)
        return remote(sums.at[to], sums_in.at[by - 1], red_s.at[p, by - 1], red_r.at[p, by - 1], moved(2, by))

    def sol_copy(level):
        at = pl.ds(level * CAP, CAP)
        return remote(sol_other.at[at], sol.at[q, at], sol_s.at[level], sol_r.at[level], partner)

    for c in range(CAP):
        for copy in phase0(0, c):
            copy.start()

    def find(level):
        for s in range(2):
            first = (row + s - 2 * s * q) * ROWS
            start = jnp.int32(0)
            for r in range(ROWS):
                start += (levels[first + r] < level).astype(jnp.int32)
            for c in range(CAP):
                r = jnp.minimum(start + c, ROWS - 1)
                rows[s * CAP + c] = r
                for k in range(SLOTS):
                    j = pattern[r, k] if s == 0 else pat_other[r, k]
                    j0 = jnp.maximum(j, 0)
                    inside = lax.rem(j0, ROWS)
                    its = levels[j0]
                    rank = ((levels[jnp.maximum(j0 - 1, 0)] == its) & (inside >= 1)).astype(jnp.int32) + (
                        (levels[jnp.maximum(j0 - 2, 0)] == its) & (inside >= 2)
                    ).astype(jnp.int32)
                    slot = (its * CAP + rank) * 32 + j0 // ROWS
                    slot = jnp.where(j < 0, EMPTY, jnp.minimum(slot, EMPTY))
                    lookup[(s * CAP + c) * SLOTS + k] = slot

    def body(level, carry):
        p = lax.rem(level - 1, 2)
        p_next = lax.rem(level, 2)
        for c in range(CAP):
            for copy in phase0_in(p, c):
                copy.wait_recv()
            for copy in phase1(p, c):
                copy.start()
        for c in range(CAP):
            for copy in phase1_in(p, c):
                copy.wait_recv()
            for k in (0, 2, 1, 3):
                phase2(p, c, k).start()

        @pl.when(level == 1)
        def _():
            for copy in start_copies():
                copy.wait()
            own[1].wait()
            own[2].wait()

        find(level)
        for c in range(CAP):
            phase2_in(p, c, 0).wait_recv()
            phase2(p, c, 4).start()
            phase2_in(p, c, 2).wait_recv()
            phase2(p, c, 5).start()
        for c in range(CAP):
            for k in (1, 3, 4, 5):
                phase2_in(p, c, k).wait_recv()
        for c in range(CAP):
            for copy in phase0(p, c) + phase1(p, c) + [phase2(p, c, k) for k in range(6)]:
                copy.wait_send()

        def to_table(i, carry):
            a, b = i // 4, lax.rem(i, 4)
            for c in range(CAP):
                at = ((level - 1) * CAP + c) * 32 + i * 2
                for e in range(4):
                    xyz = (a, b, e)
                    d0, d1, d2 = ORDERS[c]
                    from_ = xyz[d2] * 16 + xyz[d1] * 4 + xyz[d0]
                    for core in range(2):
                        table[at + core, e] = land[p, c, from_, core]
            return carry

        lax.fori_loop(0, 16, to_table, 0)

        for s in range(2):
            for c in range(CAP):
                i = s * CAP + c
                r = rows[i]
                total = None
                for k in range(SLOTS):
                    piece = table[lookup[i * SLOTS + k]].reshape(4 * W, B)
                    term = dot_t(piece, blocks[s, r, k])
                    total = term if total is None else total + term
                sums[:, i] = total.reshape(4, W, B)
        for by in (2, 1, 3):
            sums_copy(p, by).start()
        for by in (2, 1, 3):
            sums_copy(p, by).wait()

        for s in range(2):
            for c in range(CAP):
                i = s * CAP + c
                r = rows[i]
                total = (sums[z, i] + sums_in[0, i]) + (sums_in[1, i] + sums_in[2, i])
                mine = rhs[r, q] if s == 0 else rhs_other[r]
                v = times_inverse(mine - total, inv[s, r])
                if s == 0:
                    sol[q, level * CAP + c] = v
                    land[p_next, c, place(c), q] = v.astype(jnp.bfloat16)
                else:
                    sol_other[level * CAP + c] = v
                    land[p_next, c, place(c), other] = v.astype(jnp.bfloat16)

        @pl.when(level < LEV - 1)
        def _():
            for c in range(CAP):
                for copy in phase0(p_next, c):
                    copy.start()

        sol_copy(level).start()
        return carry

    lax.fori_loop(1, LEV, body, 0)

    for level in range(1, LEV):
        sol_copy(level).wait_send()
    for level in range(1, LEV):
        at = pl.ds(level * CAP, CAP)
        remote(sol_other.at[at], sol.at[other, at], sol_s.at[level], sol_r.at[level], partner).wait_recv()
    for r in range(ROWS):
        its = levels[row * ROWS + r]
        rank = jnp.int32(0)
        for back in (1, 2):
            if r >= back:
                rank += (levels[row * ROWS + r - back] == its).astype(jnp.int32)
        at = its * CAP + rank
        out[r, 0] = sol[0, at]
        out[r, 1] = sol[1, at]


def per_device(factor_blocks, pattern, levels, diag_inverse, right_side):
    rhs = jnp.swapaxes(right_side, 1, 2).reshape(ROWS, 2, W, B)
    bf, f32, dma = jnp.bfloat16, jnp.float32, pltpu.SemaphoreType.DMA
    vmem = pltpu.VMEM
    out = pl.pallas_call(
        kernel,
        out_shape=jax.ShapeDtypeStruct((ROWS, 2, W, B), f32),
        in_specs=[
            pl.BlockSpec(memory_space=pl.ANY),
            pl.BlockSpec(memory_space=pltpu.SMEM),
            pl.BlockSpec(memory_space=pltpu.SMEM),
            pl.BlockSpec(memory_space=pl.ANY),
            pl.BlockSpec(memory_space=pltpu.VMEM),
        ],
        out_specs=pl.BlockSpec(memory_space=pltpu.VMEM),
        scratch_shapes=[
            vmem((2, ROWS, SLOTS, B, B), bf),
            vmem((CAP, B, B), f32),
            vmem((2, ROWS, B, B), f32),
            vmem((ROWS, W, B), f32),
            pltpu.SMEM((ROWS, SLOTS), jnp.int32),
            vmem((EMPTY + 1, 4, W, B), bf),
            vmem((2, CAP, 64, 2, W, B), bf),
            vmem((4, 2 * CAP, W, B), f32),
            vmem((3, 2 * CAP, W, B), f32),
            vmem((2, CAP, W, B), bf),
            vmem((CAP, W, B), bf),
            vmem((2, LEV * CAP, W, B), f32),
            vmem((LEV * CAP, W, B), f32),
            pltpu.SMEM((2 * CAP * SLOTS,), jnp.int32),
            pltpu.SMEM((2 * CAP,), jnp.int32),
            dma((3,)), dma((5,)), dma((5,)),
            dma((2, 9)), dma((2, 9)), dma((2, 9)), dma((2, 9)), dma((2, 18)), dma((2, 18)),
            dma((2, 3)), dma((2, 3)), dma((LEV,)), dma((LEV,)),
        ],
        compiler_params=pltpu.CompilerParams(
            collective_id=0, has_side_effects=True, vmem_limit_bytes=48 * 1024 * 1024
        ),
    )(factor_blocks, pattern, levels, diag_inverse, rhs)
    return jnp.swapaxes(out.reshape(ROWS, 2 * W, B), 1, 2)


def solution(mesh):
    return jax.shard_map(
        per_device,
        mesh=mesh,
        in_specs=(
            P("row", "col", None, None),
            P("row", "col"),
            P(),
            P("row", None, None),
            P("row", None, "col"),
        ),
        out_specs=P("row", None, "col"),
        check_vma=False,
    )
```

time: 762 us -> 169 us (0.22)
  waiting for transfers between devices: 485 us -> 0 us
  Pallas kernels: 0 us -> 163 us
  local copies, waits for them, and re-layouts: 146 us -> 6.06 us
  blocking collectives: 63.2 us -> 0 us
  between operations: 28.2 us -> 0.01 us
  matrix products: 26.2 us -> 0 us
  other arithmetic: 9.78 us -> 0 us
    all_gather x7 -> x0, waiting for transfers between devices: 344 us -> none  [per_device(): gathered = lax.all_gather(solved_bf16, 'row', axis=0, tiled=True)]
    pallas_call x0 -> x1, Pallas kernels: none -> 163 us  [per_device(): pl.pallas_call(kernel, out_shape=jax.ShapeDtypeStruct((ROWS, 2, W, B), f3...]
    reduce_scatter x8 -> x0, waiting for transfers between devices: 140 us -> none  [per_device(): lax.psum_scatter(partial_sum, 'col', scatter_dimension=2, tiled=True)]
    gather x32 -> x0, local copies, waits for them, and re-layouts: 91.1 us -> none  [the longest x16 85.1 us: per_device(): solved_table[lookup] * present[:, :, None, None].astype(jnp.bfloat16)]
    all_gather x7 -> x0, blocking collectives: 63.2 us -> none  [per_device(): solved_bf16 = lax.all_gather(solved_bf16, 'col', axis=2, tiled=True)]
    dynamic_update_slice x7 -> x0, local copies, waits for them, and re-layouts: 34.2 us -> none  [per_device(): lax.dynamic_update_slice_in_dim(solved_table, gathered, level_now * row_c...]
    dot_general x16 -> x0, matrix products: 26.2 us -> none  [the longest x8 15.8 us: per_device(): jnp.einsum('cab,cbr->car', inverse_now, rhs_now - partial_sum, precision=...]
    broadcast_in_dim x10 -> x0, local copies, waits for them, and re-layouts: 10.3 us -> none  [the longest x1 8.86 us: per_device(): jnp.zeros((LEV * row_count * CAP, block_width, table_cols), jnp.bfloat16)]
  transfers between devices with their start and end apart: 15 -> 0, of which waited for: 15 -> 0; matrix products, arithmetic and copies ran while one was open for 2% -> 0% of each run, Pallas kernels for 0% -> 0%
where the time goes in v1:
time: 169 us
  Pallas kernels  163 us (96%)
  local copies, waits for them, and re-layouts  6.06 us (4%)
    pallas_call x1, Pallas kernels, per_device(): pl.pallas_call(kernel, out_shape=jax.ShapeDtypeStruct((ROWS, 2, W, B), f3...  163 us
    unnamed x10, local copies, waits for them, and re-layouts  6.06 us

profile of v1, /device:TPU:1, one launch (start us, length us, event | category | flops | bytes accessed | tf_op | source)
XLA Modules:
  0.0 168.7 jit_solution(2250372378487239213)
XLA Ops:
  0.0 0.8 copy.6.pattern
  0.8 0.0 copy-start
  0.8 1.7 %copy-done = bf16[16,5,128,128]{3,2,1,0:T(8,128)(2,1)S(1)} copy-done((bf16[16,5,128,128]{3,2,1,0:T(8,128)(2,1)S(1)}, bf16[16,5,128,128]{3,2,1,0:T(8,128)(2,1)}, u32[]{:S(2)}) %copy-start) | copy-done | bytes 2621464
  2.5 0.0 copy-start.1
  2.5 1.2 copy-done.1
  3.7 0.0 copy-start.2
  3.7 0.9 copy-done.2
  4.7 0.0 copy-start.3
  4.7 0.7 copy-done.3
  5.4 162.6 %shard_map.55 = f32[16,2,16,128]{3,2,1,0:T(8,128)S(1)} custom-call(bf16[16,5,128,128]{3,2,1,0:T(8,128)(2,1)S(1)} %copy-done, s32[16,5]{1,0:T(8,128)S(1)} %copy.6.pattern, s32[512]{0:T(512)S(1)} %copy-done.3, f32[16,128,128]{2,1,0:T(8,128)S(1)} %copy-done.1, f32[16,2,16,128]{3,2,1,0:T(8,128)S(1)} %bitcast.7), custom_call_target="tpu_custom_call" | custom-call | tf_op jit(solution)/shard_map/pallas_call | solution.py:290
  168.0 0.7 copy.8
Async XLA Ops:
  0.8 1.7 %copy-start = (bf16[16,5,128,128]{3,2,1,0:T(8,128)(2,1)S(1)}, bf16[16,5,128,128]{3,2,1,0:T(8,128)(2,1)}, u32[]{:S(2)}) copy-start(bf16[16,5,128,128]{3,2,1,0:T(8,128)(2,1)} %factor.1) | copy-start | bytes 7864324
  2.5 1.2 copy-start.1
  3.7 0.9 copy-start.2
  4.7 0.7 copy-start.3

commit v2 on v0

v2 whole, which is shorter than its diff:
```python
import jax
import jax.numpy as jnp
from jax import lax
from jax.experimental import pallas as pl
from jax.experimental.pallas import tpu as pltpu
from jax.sharding import PartitionSpec as P

MESH = pl.DeviceIdType.MESH
LEV = 8
CAP = 3
B = 128
W = 32
ROWS = 16
SLOTS = 5
EMPTY = (LEV - 1) * 32 * CAP
EARLY = 6
AHEAD = 3


def dot_t(a, b):
    return lax.dot_general(a, b, (((1,), (1,)), ((), ())), preferred_element_type=jnp.float32)


def split(a):
    high = a.astype(jnp.bfloat16)
    return high, (a - high.astype(jnp.float32)).astype(jnp.bfloat16)


def times_inverse(v, d):
    n = v.shape[0]
    v_high, v_low = split(v)
    d_high, d_low = split(d)
    both = dot_t(jnp.concatenate([v_high, v_low], axis=0), d_high)
    return both[:n] + (both[n:] + dot_t(v_high, d_low))


def kernel(
    factor, pattern, levels, inverse, rhs, out,
    blocks, late, inv0, inv, pats, table, land, sol, lookup, rows,
    local_sem, late_sem, pat_s, pat_r, zs, zr, gs, gr, cs, cr,
):
    row, z = lax.axis_index("row"), lax.axis_index("col")
    x, y, q = row // 8, lax.rem(row // 2, 4), lax.rem(row, 2)
    chip = x * 4 + y
    partner = (chip * 2 + 1 - q, z)

    def along_z(by):
        return (row, lax.rem(z + by, 4))

    def remote(src, dst, s, r, to):
        return pltpu.make_async_remote_copy(
            src_ref=src, dst_ref=dst, send_sem=s, recv_sem=r, device_id=to, device_id_type=MESH
        )

    own = [
        pltpu.make_async_copy(inverse.at[0:CAP], inv0, local_sem.at[0]),
        pltpu.make_async_copy(inverse, inv, local_sem.at[1]),
        pltpu.make_async_copy(factor.at[0:EARLY], blocks.at[0:EARLY, z], local_sem.at[2]),
        pltpu.make_async_copy(factor.at[EARLY:ROWS], late.at[:, z], local_sem.at[3]),
    ]
    for c in own:
        c.start()

    offsets = [(dx, dy) for dx in range(4) for dy in range(4) if (dx, dy) != (0, 0)]
    offsets.sort(key=lambda o: -(min(o[0], 4 - o[0]) + min(o[1], 4 - o[1])))

    def in_plane(dx, dy):
        return ((lax.rem(x + dx, 4) * 4 + lax.rem(y + dy, 4)) * 2 + q, z)

    barrier = pltpu.get_barrier_semaphore()
    greeted = [partner] + [along_z(by) for by in (1, 2, 3)] + [in_plane(*o) for o in offsets]
    for to in greeted:
        pl.semaphore_signal(barrier, inc=1, device_id=to, device_id_type=MESH)
    table[EMPTY] = jnp.zeros(table.shape[1:], table.dtype)
    pl.semaphore_wait(barrier, len(greeted))

    def home(t, owner):
        if isinstance(t, int) and t < EARLY:
            return blocks.at[t, owner]
        return late.at[t - EARLY, owner]

    def direct(t):
        return [remote(factor.at[t], home(t, z), zs.at[t, k], zr.at[t, k], along_z(1 + 2 * k)) for k in range(2)]

    def arrives(t, k, owner):
        unit = home(t, owner)
        return remote(unit, unit, zs.at[t, k], zr.at[t, k], along_z(1))

    def forward(t):
        by = 1 + 2 * lax.rem(t + q, 2)
        unit = home(t, lax.rem(z + 4 - by, 4))
        return remote(unit, unit, zs.at[t, 2], zr.at[t, 2], along_z(by))

    def pass_on(t):
        k = lax.rem(t + q, 2)
        arrives(t, k, lax.rem(z + 3 - 2 * k, 4)).wait_recv()
        forward(t).start()

    def send_ahead(t):
        for copy in direct(t):
            copy.start()

    def arrive(t):
        k = lax.rem(t + q, 2)
        arrives(t, 1 - k, lax.rem(z + 1 + 2 * k, 4)).wait_recv()
        arrives(t, 2, lax.rem(z + 2, 4)).wait_recv()

    for t in range(1, 1 + AHEAD):
        send_ahead(t)

    def pattern_copies():
        return [remote(pattern, pats.at[3 - by], pat_s.at[by - 1], pat_r.at[by - 1], along_z(by)) for by in (1, 2, 3)]

    def pattern_arrives():
        return [remote(pats.at[3 - by], pats.at[3 - by], pat_s.at[by - 1], pat_r.at[by - 1], along_z(by)) for by in (1, 2, 3)]

    def spread(p, dx, dy):
        unit = land.at[p, q, x, y]
        return remote(unit, unit, gs.at[p, dx, dy], gr.at[p, dx, dy], in_plane(dx, dy))

    def spread_in(p, dx, dy):
        unit = land.at[p, q, lax.rem(x + 4 - dx, 4), lax.rem(y + 4 - dy, 4)]
        return remote(unit, unit, gs.at[p, dx, dy], gr.at[p, dx, dy], in_plane(dx, dy))

    def across(p, dx, core):
        unit = land.at[p, core, lax.rem(x + 4 - dx, 4)]
        return remote(unit, unit, cs.at[p, dx], cr.at[p, dx], partner)

    def start_spread(p):
        for o in offsets:
            spread(p, *o).start()

    own[0].wait()
    for c in range(CAP):
        v = times_inverse(rhs[c], inv0[c])
        sol[c] = v
        land[0, q, x, y, c] = v.astype(jnp.bfloat16)
    start_spread(0)
    for copy in pattern_copies():
        copy.start()

    def find(level):
        first = row * ROWS
        start = jnp.int32(0)
        for r in range(ROWS):
            start += (levels[first + r] < level).astype(jnp.int32)
        for c in range(CAP):
            r = jnp.minimum(start + c, ROWS - 1)
            rows[c] = r
            for k in range(4 * SLOTS):
                far, slot = k // SLOTS, k % SLOTS
                j = pattern[r, slot] if far == 0 else pats[far - 1, r, slot]
                j0 = jnp.maximum(j, 0)
                inside = lax.rem(j0, ROWS)
                its = levels[j0]
                rank = ((levels[jnp.maximum(j0 - 1, 0)] == its) & (inside >= 1)).astype(jnp.int32) + (
                    (levels[jnp.maximum(j0 - 2, 0)] == its) & (inside >= 2)
                ).astype(jnp.int32)
                group = j0 // ROWS
                at = ((its * 2 + lax.rem(group, 2)) * 16 + group // 2) * CAP + rank
                lookup[c * 4 * SLOTS + k] = jnp.where(j < 0, EMPTY, jnp.minimum(at, EMPTY))

    def from_late(t):
        return pltpu.make_async_copy(late.at[t - EARLY], blocks.at[t], late_sem.at[t - EARLY])

    def body(level, carry):
        p = lax.rem(level - 1, 2)
        p_next = lax.rem(level, 2)

        @pl.when(level == 1)
        def _():
            pass_on(1)
            send_ahead(1 + AHEAD)

        @pl.when((level >= 2) & (level <= 4))
        def _():
            pass_on(3 * level)
            send_ahead_late(3 * level + AHEAD)

        for dx in (0, 1, 3, 2):
            for dy in (1, 3, 2, 0):
                if (dx, dy) != (0, 0):
                    spread_in(p, dx, dy).wait_recv()
            across(p, dx, q).start()

        @pl.when(level == 1)
        def _():
            for copy in pattern_arrives():
                copy.wait_recv()
            for copy in pattern_copies():
                copy.wait_send()

        find(level)

        @pl.when(level == 1)
        def _():
            for t in range(2, EARLY):
                pass_on(t)
                send_ahead(t + AHEAD)
            for t in range(1, EARLY):
                arrive(t)
            for copy in own[1:]:
                copy.wait()

        @pl.when((level >= 2) & (level <= 4))
        def _():
            for i in (1, 2):
                pass_on(3 * level + i)
                send_ahead_late(3 * level + i + AHEAD)
            for i in range(3):
                arrive(3 * level + i)
                from_late(3 * level + i).start()

        @pl.when(level == 5)
        def _():
            pass_on(jnp.int32(15))
            arrive(jnp.int32(15))
            from_late(jnp.int32(15)).start()

        for o in offsets:
            spread(p, *o).wait_send()
        for dx in range(4):
            across(p, dx, q).wait_send()
            across(p, dx, 1 - q).wait_recv()

        def to_table(i, carry):
            a, b = i // 4, lax.rem(i, 4)
            for core in range(2):
                for c in range(CAP):
                    table[(((level - 1) * 2 + core) * 16 + i) * CAP + c] = land[p, core, a, b, c]
            return carry

        lax.fori_loop(0, 16, to_table, 0)

        @pl.when((level >= 2) & (level <= 4))
        def _():
            for i in range(3):
                from_late(3 * level + i).wait()

        @pl.when(level == 5)
        def _():
            from_late(jnp.int32(15)).wait()

        for c in range(CAP):
            r = rows[c]
            total = None
            for k in range(0, 4 * SLOTS, 2):
                pieces = [table[lookup[c * 4 * SLOTS + k + i]] for i in range(2)]
                factors = [blocks[r, lax.rem(z + (k + i) // SLOTS, 4), (k + i) % SLOTS] for i in range(2)]
                term = dot_t(jnp.concatenate(pieces, axis=1), jnp.concatenate(factors, axis=1))
                total = term if total is None else total + term
            v = times_inverse(rhs[r] - total, inv[r])
            sol[level * CAP + c] = v
            land[p_next, q, x, y, c] = v.astype(jnp.bfloat16)

        @pl.when(level < LEV - 1)
        def _():
            start_spread(p_next)

        return carry

    def send_ahead_late(t):
        @pl.when(t <= ROWS - 1)
        def _():
            send_ahead(t)

    lax.fori_loop(1, LEV, body, 0)

    for t in range(1, ROWS):
        for copy in direct(t) + [forward(t)]:
            copy.wait_send()
    for r in range(ROWS):
        its = levels[row * ROWS + r]
        rank = jnp.int32(0)
        for back in (1, 2):
            if r >= back:
                rank += (levels[row * ROWS + r - back] == its).astype(jnp.int32)
        out[r] = sol[its * CAP + rank]


def per_device(factor_blocks, pattern, levels, diag_inverse, right_side):
    rhs = jnp.swapaxes(right_side, 1, 2)
    bf, f32, dma = jnp.bfloat16, jnp.float32, pltpu.SemaphoreType.DMA
    vmem = pltpu.VMEM
    out = pl.pallas_call(
        kernel,
        out_shape=jax.ShapeDtypeStruct((ROWS, W, B), f32),
        in_specs=[
            pl.BlockSpec(memory_space=pl.ANY),
            pl.BlockSpec(memory_space=pltpu.SMEM),
            pl.BlockSpec(memory_space=pltpu.SMEM),
            pl.BlockSpec(memory_space=pl.ANY),
            pl.BlockSpec(memory_space=pltpu.VMEM),
        ],
        out_specs=pl.BlockSpec(memory_space=pltpu.VMEM),
        scratch_shapes=[
            vmem((ROWS, 4, SLOTS, B, B), bf),
            vmem((ROWS - EARLY, 4, SLOTS, B, B), bf),
            vmem((CAP, B, B), f32),
            vmem((ROWS, B, B), f32),
            pltpu.SMEM((3, ROWS, SLOTS), jnp.int32),
            vmem((EMPTY + 1, W, B), bf),
            vmem((2, 2, 4, 4, CAP, W, B), bf),
            vmem((LEV * CAP, W, B), f32),
            pltpu.SMEM((CAP * 4 * SLOTS,), jnp.int32),
            pltpu.SMEM((CAP,), jnp.int32),
            dma((4,)), dma((ROWS - EARLY,)), dma((3,)), dma((3,)),
            dma((ROWS, 3)), dma((ROWS, 3)),
            dma((2, 4, 4)), dma((2, 4, 4)), dma((2, 4)), dma((2, 4)),
        ],
        compiler_params=pltpu.CompilerParams(
            collective_id=0, has_side_effects=True, vmem_limit_bytes=56 * 1024 * 1024
        ),
    )(factor_blocks, pattern, levels, diag_inverse, rhs)
    return jnp.swapaxes(out, 1, 2)


def solution(mesh):
    return jax.shard_map(
        per_device,
        mesh=mesh,
        in_specs=(
            P("row", "col", None, None),
            P("row", "col"),
            P(),
            P("row", None, None),
            P("row", None, "col"),
        ),
        out_specs=P("row", None, "col"),
        check_vma=False,
    )
```

time: 762 us -> 139 us (0.18)
  waiting for transfers between devices: 485 us -> 0 us
  local copies, waits for them, and re-layouts: 146 us -> 3.03 us
  Pallas kernels: 0 us -> 136 us
  blocking collectives: 63.2 us -> 0 us
  between operations: 28.2 us -> 0.01 us
  matrix products: 26.2 us -> 0 us
  other arithmetic: 9.78 us -> 0 us
    all_gather x7 -> x0, waiting for transfers between devices: 344 us -> none  [per_device(): gathered = lax.all_gather(solved_bf16, 'row', axis=0, tiled=True)]
    reduce_scatter x8 -> x0, waiting for transfers between devices: 140 us -> none  [per_device(): lax.psum_scatter(partial_sum, 'col', scatter_dimension=2, tiled=True)]
    pallas_call x0 -> x1, Pallas kernels: none -> 136 us  [per_device(): pl.pallas_call(kernel, out_shape=jax.ShapeDtypeStruct((ROWS, W, B), f32),...]
    gather x32 -> x0, local copies, waits for them, and re-layouts: 91.1 us -> none  [the longest x16 85.1 us: per_device(): solved_table[lookup] * present[:, :, None, None].astype(jnp.bfloat16)]
    all_gather x7 -> x0, blocking collectives: 63.2 us -> none  [per_device(): solved_bf16 = lax.all_gather(solved_bf16, 'col', axis=2, tiled=True)]
    dynamic_update_slice x7 -> x0, local copies, waits for them, and re-layouts: 34.2 us -> none  [per_device(): lax.dynamic_update_slice_in_dim(solved_table, gathered, level_now * row_c...]
    dot_general x16 -> x0, matrix products: 26.2 us -> none  [the longest x8 15.8 us: per_device(): jnp.einsum('cab,cbr->car', inverse_now, rhs_now - partial_sum, precision=...]
    broadcast_in_dim x10 -> x0, local copies, waits for them, and re-layouts: 10.3 us -> none  [the longest x1 8.86 us: per_device(): jnp.zeros((LEV * row_count * CAP, block_width, table_cols), jnp.bfloat16)]
  transfers between devices with their start and end apart: 15 -> 0, of which waited for: 15 -> 0; matrix products, arithmetic and copies ran while one was open for 2% -> 0% of each run, Pallas kernels for 0% -> 0%
where the time goes in v2:
time: 139 us
  Pallas kernels  136 us (98%)
  local copies, waits for them, and re-layouts  3.03 us (2%)
    pallas_call x1, Pallas kernels, per_device(): pl.pallas_call(kernel, out_shape=jax.ShapeDtypeStruct((ROWS, W, B), f32),...  136 us
    unnamed x2, local copies, waits for them, and re-layouts  3.03 us

profile of v2, /device:TPU:1, one launch (start us, length us, event | category | flops | bytes accessed | tf_op | source)
XLA Modules:
  0.0 139.3 jit_solution(8172163612397801346)
XLA Ops:
  0.0 1.4 copy.6.pattern
  1.4 136.3 %shard_map.55 = f32[16,32,128]{2,1,0:T(8,128)} custom-call(bf16[16,5,128,128]{3,2,1,0:T(8,128)(2,1)} %factor.1, s32[16,5]{1,0:T(8,128)} %copy.6.pattern, s32[512]{0:T(512)} %levels.1, f32[16,128,128]{2,1,0:T(8,128)} %inverse.1, f32[16,32,128]{2,1,0:T(8,128)} %bitcast.3), custom_call_target="tpu_custom_call" | custom-call | tf_op jit(solution)/shard_map/pallas_call | solution.py:285
  137.6 1.7 %copy.8 = f32[16,128,32]{1,2,0:T(8,128)} copy(f32[16,128,32]{1,2,0:T(8,128)} %bitcast.2) | data formatting | bytes 524288

commit v3 on v2

--- a/solution.py
+++ b/solution.py
@@ -105,14 +105,16 @@
         arrives(t, 1 - k, lax.rem(z + 1 + 2 * k, 4)).wait_recv()
         arrives(t, 2, lax.rem(z + 2, 4)).wait_recv()
 
+    def pattern_copies():
+        return [remote(pattern, pats.at[3 - by], pat_s.at[by - 1], pat_r.at[by - 1], along_z(by)) for by in (1, 2, 3)]
+
+    def pattern_arrives():
+        return [remote(pats.at[3 - by], pats.at[3 - by], pat_s.at[by - 1], pat_r.at[by - 1], along_z(by)) for by in (1, 2, 3)]
+
+    for copy in pattern_copies():
+        copy.start()
     for t in range(1, 1 + AHEAD):
         send_ahead(t)
-
-    def pattern_copies():
-        return [remote(pattern, pats.at[3 - by], pat_s.at[by - 1], pat_r.at[by - 1], along_z(by)) for by in (1, 2, 3)]
-
-    def pattern_arrives():
-        return [remote(pats.at[3 - by], pats.at[3 - by], pat_s.at[by - 1], pat_r.at[by - 1], along_z(by)) for by in (1, 2, 3)]
 
     def spread(p, dx, dy):
         unit = land.at[p, q, x, y]
@@ -136,8 +138,6 @@
         sol[c] = v
         land[0, q, x, y, c] = v.astype(jnp.bfloat16)
     start_spread(0)
-    for copy in pattern_copies():
-        copy.start()
 
     def find(level):
         first = row * ROWS
@@ -171,26 +171,28 @@
         def _():
             pass_on(1)
             send_ahead(1 + AHEAD)
-
-        @pl.when((level >= 2) & (level <= 4))
+            for copy in pattern_arrives():
+                copy.wait_recv()
+            for copy in pattern_copies():
+                copy.wait_send()
+
+        find(level)
+
+        @pl.when((level == 2) | (level == 3))
         def _():
             pass_on(3 * level)
             send_ahead_late(3 * level + AHEAD)
+
+        @pl.when((level == 4) | (level == 5))
+        def _():
+            pass_on(2 * level + 4)
+            send_ahead_late(2 * level + 4 + AHEAD)
 
         for dx in (0, 1, 3, 2):
             for dy in (1, 3, 2, 0):
                 if (dx, dy) != (0, 0):
                     spread_in(p, dx, dy).wait_recv()
             across(p, dx, q).start()
-
-        @pl.when(level == 1)
-        def _():
-            for copy in pattern_arrives():
-                copy.wait_recv()
-            for copy in pattern_copies():
-                copy.wait_send()
-
-        find(level)
 
         @pl.when(level == 1)
         def _():
@@ -202,7 +204,7 @@
             for copy in own[1:]:
                 copy.wait()
 
-        @pl.when((level >= 2) & (level <= 4))
+        @pl.when((level == 2) | (level == 3))
         def _():
             for i in (1, 2):
                 pass_on(3 * level + i)
@@ -211,11 +213,14 @@
                 arrive(3 * level + i)
                 from_late(3 * level + i).start()
 
-        @pl.when(level == 5)
-        def _():
-            pass_on(jnp.int32(15))
-            arrive(jnp.int32(15))
-            from_late(jnp.int32(15)).start()
+        @pl.when((level == 4) | (level == 5))
+        def _():
+            pass_on(2 * level + 5)
+
+        @pl.when(level >= 4)
+        def _():
+            arrive(level + 8)
+            from_late(level + 8).start()
 
         for o in offsets:
             spread(p, *o).wait_send()
@@ -232,14 +237,14 @@
 
         lax.fori_loop(0, 16, to_table, 0)
 
-        @pl.when((level >= 2) & (level <= 4))
+        @pl.when((level == 2) | (level == 3))
         def _():
             for i in range(3):
                 from_late(3 * level + i).wait()
 
-        @pl.when(level == 5)
-        def _():
-            from_late(jnp.int32(15)).wait()
+        @pl.when(level >= 4)
+        def _():
+            from_late(level + 8).wait()
 
         for c in range(CAP):
             r = rows[c]

time: 139 us -> 130 us (0.935)
  Pallas kernels: 136 us -> 127 us
    pallas_call x1, Pallas kernels: 136 us -> 127 us  [per_device(): pl.pallas_call(kernel, out_shape=jax.ShapeDtypeStruct((ROWS, W, B), f32),...]
where the time goes in v3:
time: 130 us
  Pallas kernels  127 us (98%)
  local copies, waits for them, and re-layouts  3.03 us (2%)
    pallas_call x1, Pallas kernels, per_device(): pl.pallas_call(kernel, out_shape=jax.ShapeDtypeStruct((ROWS, W, B), f32),...  127 us
    unnamed x2, local copies, waits for them, and re-layouts  3.03 us

profile of v3, /device:TPU:1, one launch (start us, length us, event | category | flops | bytes accessed | tf_op | source)
XLA Modules:
  0.0 129.9 jit_solution(2921748225666670714)
XLA Ops:
  0.0 1.4 %copy.6.pattern = s32[16,5]{1,0:T(8,128)} copy(s32[16,5]{0,1:T(8,128)} %param.6) | data formatting | bytes 640 | tf_op args[1]
  1.4 126.8 %shard_map.55 = f32[16,32,128]{2,1,0:T(8,128)} custom-call(bf16[16,5,128,128]{3,2,1,0:T(8,128)(2,1)} %factor.1, s32[16,5]{1,0:T(8,128)} %copy.6.pattern, s32[512]{0:T(512)} %levels.1, f32[16,128,128]{2,1,0:T(8,128)} %inverse.1, f32[16,32,128]{2,1,0:T(8,128)} %bitcast.3), custom_call_target="tpu_custom_call" | custom-call | tf_op jit(solution)/shard_map/pallas_call | solution.py:290
  128.2 1.7 %copy.8 = f32[16,128,32]{1,2,0:T(8,128)} copy(f32[16,128,32]{1,2,0:T(8,128)} %bitcast.2) | data formatting | bytes 524288

commit v4 on v3

--- a/solution.py
+++ b/solution.py
@@ -14,7 +14,7 @@
 SLOTS = 5
 EMPTY = (LEV - 1) * 32 * CAP
 EARLY = 6
-AHEAD = 3
+AHEAD = 2
 
 
 def dot_t(a, b):
@@ -181,12 +181,14 @@
         @pl.when((level == 2) | (level == 3))
         def _():
             pass_on(3 * level)
-            send_ahead_late(3 * level + AHEAD)
 
         @pl.when((level == 4) | (level == 5))
         def _():
             pass_on(2 * level + 4)
-            send_ahead_late(2 * level + 4 + AHEAD)
+
+        @pl.when(level == 4)
+        def _():
+            send_ahead(jnp.int32(14))
 
         for dx in (0, 1, 3, 2):
             for dy in (1, 3, 2, 0):
@@ -198,9 +200,13 @@
         def _():
             for t in range(2, EARLY):
                 pass_on(t)
-                send_ahead(t + AHEAD)
+                if t + AHEAD < EARLY:
+                    send_ahead(t + AHEAD)
+            send_ahead(EARLY)
             for t in range(1, EARLY):
                 arrive(t)
+            send_ahead(EARLY + 1)
+            send_ahead(EARLY + 2)
             for copy in own[1:]:
                 copy.wait()
 
@@ -208,14 +214,23 @@
         def _():
             for i in (1, 2):
                 pass_on(3 * level + i)
-                send_ahead_late(3 * level + i + AHEAD)
+            send_ahead(3 * level + 3)
             for i in range(3):
                 arrive(3 * level + i)
                 from_late(3 * level + i).start()
+            send_ahead(3 * level + 4)
+
+            @pl.when(level == 2)
+            def _():
+                send_ahead(jnp.int32(11))
 
         @pl.when((level == 4) | (level == 5))
         def _():
             pass_on(2 * level + 5)
+
+        @pl.when(level == 4)
+        def _():
+            send_ahead(jnp.int32(15))
 
         @pl.when(level >= 4)
         def _():
@@ -263,11 +278,6 @@
             start_spread(p_next)
 
         return carry
-
-    def send_ahead_late(t):
-        @pl.when(t <= ROWS - 1)
-        def _():
-            send_ahead(t)
 
     lax.fori_loop(1, LEV, body, 0)
 

time: 130 us -> 121 us (0.931)
  Pallas kernels: 127 us -> 118 us
    pallas_call x1, Pallas kernels: 127 us -> 118 us  [per_device(): pl.pallas_call(kernel, out_shape=jax.ShapeDtypeStruct((ROWS, W, B), f32),...]
where the time goes in v4:
time: 121 us
  Pallas kernels  118 us (98%)
  local copies, waits for them, and re-layouts  3.03 us (3%)
    pallas_call x1, Pallas kernels, per_device(): pl.pallas_call(kernel, out_shape=jax.ShapeDtypeStruct((ROWS, W, B), f32),...  118 us
    unnamed x2, local copies, waits for them, and re-layouts  3.03 us

profile of v4, /device:TPU:1, one launch (start us, length us, event | category | flops | bytes accessed | tf_op | source)
XLA Modules:
  0.0 120.6 jit_solution(6475212478929324494)
XLA Ops:
  0.0 1.4 %copy.6.pattern = s32[16,5]{1,0:T(8,128)} copy(s32[16,5]{0,1:T(8,128)} %param.6) | data formatting | bytes 640 | tf_op args[1]
  1.4 117.6 %shard_map.55 = f32[16,32,128]{2,1,0:T(8,128)} custom-call(bf16[16,5,128,128]{3,2,1,0:T(8,128)(2,1)} %factor.1, s32[16,5]{1,0:T(8,128)} %copy.6.pattern, s32[512]{0:T(512)} %levels.1, f32[16,128,128]{2,1,0:T(8,128)} %inverse.1, f32[16,32,128]{2,1,0:T(8,128)} %bitcast.3), custom_call_target="tpu_custom_call" | custom-call | tf_op jit(solution)/shard_map/pallas_call | solution.py:300
  118.9 1.7 %copy.8 = f32[16,128,32]{1,2,0:T(8,128)} copy(f32[16,128,32]{1,2,0:T(8,128)} %bitcast.2) | data formatting | bytes 524288

commit v5 on v3

--- a/solution.py
+++ b/solution.py
@@ -13,8 +13,9 @@
 ROWS = 16
 SLOTS = 5
 EMPTY = (LEV - 1) * 32 * CAP
-EARLY = 6
-AHEAD = 3
+SENT = ROWS - 1
+EARLY = 3
+AHEAD = 2
 
 
 def dot_t(a, b):
@@ -26,17 +27,20 @@
     return high, (a - high.astype(jnp.float32)).astype(jnp.bfloat16)
 
 
+def both_terms(d):
+    return jnp.concatenate(split(d), axis=0)
+
+
 def times_inverse(v, d):
     n = v.shape[0]
     v_high, v_low = split(v)
-    d_high, d_low = split(d)
-    both = dot_t(jnp.concatenate([v_high, v_low], axis=0), d_high)
-    return both[:n] + (both[n:] + dot_t(v_high, d_low))
+    terms = dot_t(jnp.concatenate([v_high, v_low], axis=0), d)
+    return terms[:n, :B] + (terms[n:, :B] + terms[:n, B:])
 
 
 def kernel(
-    factor, pattern, levels, inverse, rhs, out,
-    blocks, late, inv0, inv, pats, table, land, sol, lookup, rows,
+    factor, pattern, levels, inverse, right, out,
+    raw, blocks, late, inv0, inv, inv_terms, right_in, rhs, pats, table, land, sol, lookup, rows, places,
     local_sem, late_sem, pat_s, pat_r, zs, zr, gs, gr, cs, cr,
 ):
     row, z = lax.axis_index("row"), lax.axis_index("col")
@@ -55,11 +59,12 @@
     own = [
         pltpu.make_async_copy(inverse.at[0:CAP], inv0, local_sem.at[0]),
         pltpu.make_async_copy(inverse, inv, local_sem.at[1]),
-        pltpu.make_async_copy(factor.at[0:EARLY], blocks.at[0:EARLY, z], local_sem.at[2]),
-        pltpu.make_async_copy(factor.at[EARLY:ROWS], late.at[:, z], local_sem.at[3]),
+        pltpu.make_async_copy(factor, raw, local_sem.at[2]),
+        pltpu.make_async_copy(right.at[0:CAP], right_in.at[0:CAP], local_sem.at[3]),
+        pltpu.make_async_copy(right.at[CAP:ROWS], right_in.at[CAP:ROWS], local_sem.at[4]),
     ]
-    for c in own:
-        c.start()
+    for i in (0, 3, 2, 1, 4):
+        own[i].start()
 
     offsets = [(dx, dy) for dx in range(4) for dy in range(4) if (dx, dy) != (0, 0)]
     offsets.sort(key=lambda o: -(min(o[0], 4 - o[0]) + min(o[1], 4 - o[1])))
@@ -72,6 +77,26 @@
     for to in greeted:
         pl.semaphore_signal(barrier, inc=1, device_id=to, device_id_type=MESH)
     table[EMPTY] = jnp.zeros(table.shape[1:], table.dtype)
+
+    def count_below(level):
+        count = jnp.int32(0)
+        for r in range(ROWS):
+            count += (levels[row * ROWS + r] < level).astype(jnp.int32)
+        return count
+
+    skipped = count_below(1)
+    own[3].wait()
+    for r in range(CAP):
+        rhs[r] = jnp.swapaxes(right_in[r], 0, 1)
+    own[2].wait()
+    for n in range(EARLY):
+        blocks[n, z] = raw[jnp.minimum(skipped + n, ROWS - 1)]
+
+    def shift(n, carry):
+        late[n - EARLY, z] = raw[jnp.minimum(skipped + n, ROWS - 1)]
+        return carry
+
+    lax.fori_loop(EARLY, SENT, shift, 0)
     pl.semaphore_wait(barrier, len(greeted))
 
     def home(t, owner):
@@ -80,7 +105,7 @@
         return late.at[t - EARLY, owner]
 
     def direct(t):
-        return [remote(factor.at[t], home(t, z), zs.at[t, k], zr.at[t, k], along_z(1 + 2 * k)) for k in range(2)]
+        return [remote(home(t, z), home(t, z), zs.at[t, k], zr.at[t, k], along_z(1 + 2 * k)) for k in range(2)]
 
     def arrives(t, k, owner):
         unit = home(t, owner)
@@ -113,7 +138,7 @@
 
     for copy in pattern_copies():
         copy.start()
-    for t in range(1, 1 + AHEAD):
+    for t in range(AHEAD):
         send_ahead(t)
 
     def spread(p, dx, dy):
@@ -134,19 +159,26 @@
 
     own[0].wait()
     for c in range(CAP):
-        v = times_inverse(rhs[c], inv0[c])
+        v = times_inverse(rhs[c], both_terms(inv0[c]))
         sol[c] = v
         land[0, q, x, y, c] = v.astype(jnp.bfloat16)
     start_spread(0)
+    own[1].wait()
+    own[4].wait()
+
+    def prepare(r, carry):
+        inv_terms[r] = both_terms(inv[r])
+        rhs[r] = jnp.swapaxes(right_in[r], 0, 1)
+        return carry
+
+    lax.fori_loop(0, ROWS, prepare, 0)
 
     def find(level):
-        first = row * ROWS
-        start = jnp.int32(0)
-        for r in range(ROWS):
-            start += (levels[first + r] < level).astype(jnp.int32)
+        start = count_below(level)
         for c in range(CAP):
             r = jnp.minimum(start + c, ROWS - 1)
             rows[c] = r
+            places[c] = jnp.clip(r - skipped, 0, SENT - 1)
             for k in range(4 * SLOTS):
                 far, slot = k // SLOTS, k % SLOTS
                 j = pattern[r, slot] if far == 0 else pats[far - 1, r, slot]
@@ -169,8 +201,8 @@
 
         @pl.when(level == 1)
         def _():
-            pass_on(1)
-            send_ahead(1 + AHEAD)
+            pass_on(0)
+            send_ahead(AHEAD)
             for copy in pattern_arrives():
                 copy.wait_recv()
             for copy in pattern_copies():
@@ -178,15 +210,13 @@
 
         find(level)
 
-        @pl.when((level == 2) | (level == 3))
-        def _():
-            pass_on(3 * level)
-            send_ahead_late(3 * level + AHEAD)
-
-        @pl.when((level == 4) | (level == 5))
-        def _():
-            pass_on(2 * level + 4)
-            send_ahead_late(2 * level + 4 + AHEAD)
+        @pl.when((level >= 2) & (level <= 4))
+        def _():
+            pass_on(3 * level - 3)
+
+        @pl.when((level == 5) | (level == 6))
+        def _():
+            pass_on(2 * level + 2)
 
         for dx in (0, 1, 3, 2):
             for dy in (1, 3, 2, 0):
@@ -196,31 +226,33 @@
 
         @pl.when(level == 1)
         def _():
-            for t in range(2, EARLY):
+            for t in range(1, EARLY):
                 pass_on(t)
-                send_ahead(t + AHEAD)
-            for t in range(1, EARLY):
+            send_ahead(EARLY)
+            for t in range(EARLY):
                 arrive(t)
-            for copy in own[1:]:
-                copy.wait()
-
-        @pl.when((level == 2) | (level == 3))
+            send_ahead(EARLY + 1)
+            send_ahead(EARLY + 2)
+
+        @pl.when((level >= 2) & (level <= 4))
         def _():
             for i in (1, 2):
-                pass_on(3 * level + i)
-                send_ahead_late(3 * level + i + AHEAD)
+                pass_on(3 * level - 3 + i)
+            send_ahead(3 * level)
             for i in range(3):
-                arrive(3 * level + i)
-                from_late(3 * level + i).start()
-
-        @pl.when((level == 4) | (level == 5))
-        def _():
-            pass_on(2 * level + 5)
-
-        @pl.when(level >= 4)
-        def _():
-            arrive(level + 8)
-            from_late(level + 8).start()
+                arrive(3 * level - 3 + i)
+                from_late(3 * level - 3 + i).start()
+            send_ahead(3 * level + 1)
+            send_ahead(3 * level + 2)
+
+        @pl.when(level == 5)
+        def _():
+            pass_on(jnp.int32(13))
+
+        @pl.when(level >= 5)
+        def _():
+            arrive(level + 7)
+            from_late(level + 7).start()
 
         for o in offsets:
             spread(p, *o).wait_send()
@@ -237,24 +269,24 @@
 
         lax.fori_loop(0, 16, to_table, 0)
 
-        @pl.when((level == 2) | (level == 3))
+        @pl.when((level >= 2) & (level <= 4))
         def _():
             for i in range(3):
-                from_late(3 * level + i).wait()
-
-        @pl.when(level >= 4)
-        def _():
-            from_late(level + 8).wait()
+                from_late(3 * level - 3 + i).wait()
+
+        @pl.when(level >= 5)
+        def _():
+            from_late(level + 7).wait()
 
         for c in range(CAP):
             r = rows[c]
             total = None
             for k in range(0, 4 * SLOTS, 2):
                 pieces = [table[lookup[c * 4 * SLOTS + k + i]] for i in range(2)]
-                factors = [blocks[r, lax.rem(z + (k + i) // SLOTS, 4), (k + i) % SLOTS] for i in range(2)]
+                factors = [blocks[places[c], lax.rem(z + (k + i) // SLOTS, 4), (k + i) % SLOTS] for i in range(2)]
                 term = dot_t(jnp.concatenate(pieces, axis=1), jnp.concatenate(factors, axis=1))
                 total = term if total is None else total + term
-            v = times_inverse(rhs[r] - total, inv[r])
+            v = times_inverse(rhs[r] - total, inv_terms[r])
             sol[level * CAP + c] = v
             land[p_next, q, x, y, c] = v.astype(jnp.bfloat16)
 
@@ -264,14 +296,9 @@
 
         return carry
 
-    def send_ahead_late(t):
-        @pl.when(t <= ROWS - 1)
-        def _():
-            send_ahead(t)
-
     lax.fori_loop(1, LEV, body, 0)
 
-    for t in range(1, ROWS):
+    for t in range(SENT):
         for copy in direct(t) + [forward(t)]:
             copy.wait_send()
     for r in range(ROWS):
@@ -284,7 +311,6 @@
 
 
 def per_device(factor_blocks, pattern, levels, diag_inverse, right_side):
-    rhs = jnp.swapaxes(right_side, 1, 2)
     bf, f32, dma = jnp.bfloat16, jnp.float32, pltpu.SemaphoreType.DMA
     vmem = pltpu.VMEM
     out = pl.pallas_call(
@@ -295,28 +321,33 @@
             pl.BlockSpec(memory_space=pltpu.SMEM),
             pl.BlockSpec(memory_space=pltpu.SMEM),
             pl.BlockSpec(memory_space=pl.ANY),
-            pl.BlockSpec(memory_space=pltpu.VMEM),
+            pl.BlockSpec(memory_space=pl.ANY),
         ],
         out_specs=pl.BlockSpec(memory_space=pltpu.VMEM),
         scratch_shapes=[
-            vmem((ROWS, 4, SLOTS, B, B), bf),
-            vmem((ROWS - EARLY, 4, SLOTS, B, B), bf),
+            vmem((ROWS, SLOTS, B, B), bf),
+            vmem((SENT, 4, SLOTS, B, B), bf),
+            vmem((SENT - EARLY, 4, SLOTS, B, B), bf),
             vmem((CAP, B, B), f32),
             vmem((ROWS, B, B), f32),
+            vmem((ROWS, 2 * B, B), bf),
+            vmem((ROWS, B, W), f32),
+            vmem((ROWS, W, B), f32),
             pltpu.SMEM((3, ROWS, SLOTS), jnp.int32),
             vmem((EMPTY + 1, W, B), bf),
             vmem((2, 2, 4, 4, CAP, W, B), bf),
             vmem((LEV * CAP, W, B), f32),
             pltpu.SMEM((CAP * 4 * SLOTS,), jnp.int32),
             pltpu.SMEM((CAP,), jnp.int32),
-            dma((4,)), dma((ROWS - EARLY,)), dma((3,)), dma((3,)),
-            dma((ROWS, 3)), dma((ROWS, 3)),
+            pltpu.SMEM((CAP,), jnp.int32),
+            dma((5,)), dma((SENT - EARLY,)), dma((3,)), dma((3,)),
+            dma((SENT, 3)), dma((SENT, 3)),
             dma((2, 4, 4)), dma((2, 4, 4)), dma((2, 4)), dma((2, 4)),
         ],
         compiler_params=pltpu.CompilerParams(
             collective_id=0, has_side_effects=True, vmem_limit_bytes=56 * 1024 * 1024
         ),
-    )(factor_blocks, pattern, levels, diag_inverse, rhs)
+    )(factor_blocks, pattern, levels, diag_inverse, right_side)
     return jnp.swapaxes(out, 1, 2)
 
 

time: 130 us -> 119 us (0.915)
  Pallas kernels: 127 us -> 113 us
  local copies, waits for them, and re-layouts: 3.03 us -> 5.31 us
    pallas_call x1, Pallas kernels: 127 us -> 113 us  [per_device(): pl.pallas_call(kernel, out_shape=jax.ShapeDtypeStruct((ROWS, W, B), f32),...]
    unnamed x2 -> x3, local copies, waits for them, and re-layouts: 3.03 us -> 5.31 us
where the time goes in v5:
time: 119 us
  Pallas kernels  113 us (95%)
  local copies, waits for them, and re-layouts  5.31 us (4%)
    pallas_call x1, Pallas kernels, per_device(): pl.pallas_call(kernel, out_shape=jax.ShapeDtypeStruct((ROWS, W, B), f32),...  113 us
    unnamed x3, local copies, waits for them, and re-layouts  5.31 us

profile of v5, /device:TPU:1, one launch (start us, length us, event | category | flops | bytes accessed | tf_op | source)
XLA Modules:
  0.0 118.8 jit_solution(11115709683896015408)
XLA Ops:
  0.0 1.4 %copy.6.pattern = s32[16,5]{1,0:T(8,128)} copy(s32[16,5]{0,1:T(8,128)} %param.6) | data formatting | bytes 640 | tf_op args[1]
  1.4 2.3 %copy.7.right = f32[16,128,32]{2,1,0:T(8,128)} copy(f32[16,128,32]{1,2,0:T(8,128)} %param.9) | data formatting | bytes 524288 | tf_op args[4]
  3.6 113.5 %shard_map.55 = f32[16,32,128]{2,1,0:T(8,128)} custom-call(bf16[16,5,128,128]{3,2,1,0:T(8,128)(2,1)} %factor.1, s32[16,5]{1,0:T(8,128)} %copy.6.pattern, s32[512]{0:T(512)} %levels.1, f32[16,128,128]{2,1,0:T(8,128)} %inverse.1, f32[16,128,32]{2,1,0:T(8,128)} %copy.7.right), custom_call_target="tpu_custom_call" | custom-call | tf_op jit(solution)/shard_map/pallas_call | solution.py:316
  117.1 1.7 %copy.9 = f32[16,128,32]{1,2,0:T(8,128)} copy(f32[16,128,32]{1,2,0:T(8,128)} %bitcast.1) | data formatting | bytes 524288

commit v6 on v5

--- a/solution.py
+++ b/solution.py
@@ -40,7 +40,7 @@
 
 def kernel(
     factor, pattern, levels, inverse, right, out,
-    raw, blocks, late, inv0, inv, inv_terms, right_in, rhs, pats, table, land, sol, lookup, rows, places,
+    raw, blocks, late, inv0, inv, inv_terms, rhs, pats, table, land, sol, lookup, rows, places,
     local_sem, late_sem, pat_s, pat_r, zs, zr, gs, gr, cs, cr,
 ):
     row, z = lax.axis_index("row"), lax.axis_index("col")
@@ -60,10 +60,10 @@
         pltpu.make_async_copy(inverse.at[0:CAP], inv0, local_sem.at[0]),
         pltpu.make_async_copy(inverse, inv, local_sem.at[1]),
         pltpu.make_async_copy(factor, raw, local_sem.at[2]),
-        pltpu.make_async_copy(right.at[0:CAP], right_in.at[0:CAP], local_sem.at[3]),
-        pltpu.make_async_copy(right.at[CAP:ROWS], right_in.at[CAP:ROWS], local_sem.at[4]),
+        pltpu.make_async_copy(right.at[0:CAP], rhs.at[0:CAP], local_sem.at[3]),
+        pltpu.make_async_copy(right.at[CAP:ROWS], rhs.at[CAP:ROWS], local_sem.at[4]),
     ]
-    for i in (0, 3, 2, 1, 4):
+    for i in (2, 0, 3, 1, 4):
         own[i].start()
 
     offsets = [(dx, dy) for dx in range(4) for dy in range(4) if (dx, dy) != (0, 0)]
@@ -85,9 +85,6 @@
         return count
 
     skipped = count_below(1)
-    own[3].wait()
-    for r in range(CAP):
-        rhs[r] = jnp.swapaxes(right_in[r], 0, 1)
     own[2].wait()
     for n in range(EARLY):
         blocks[n, z] = raw[jnp.minimum(skipped + n, ROWS - 1)]
@@ -158,6 +155,7 @@
             spread(p, *o).start()
 
     own[0].wait()
+    own[3].wait()
     for c in range(CAP):
         v = times_inverse(rhs[c], both_terms(inv0[c]))
         sol[c] = v
@@ -168,7 +166,6 @@
 
     def prepare(r, carry):
         inv_terms[r] = both_terms(inv[r])
-        rhs[r] = jnp.swapaxes(right_in[r], 0, 1)
         return carry
 
     lax.fori_loop(0, ROWS, prepare, 0)
@@ -181,7 +178,7 @@
             places[c] = jnp.clip(r - skipped, 0, SENT - 1)
             for k in range(4 * SLOTS):
                 far, slot = k // SLOTS, k % SLOTS
-                j = pattern[r, slot] if far == 0 else pats[far - 1, r, slot]
+                j = pattern[slot, r] if far == 0 else pats[far - 1, slot, r]
                 j0 = jnp.maximum(j, 0)
                 inside = lax.rem(j0, ROWS)
                 its = levels[j0]
@@ -331,9 +328,8 @@
             vmem((CAP, B, B), f32),
             vmem((ROWS, B, B), f32),
             vmem((ROWS, 2 * B, B), bf),
-            vmem((ROWS, B, W), f32),
             vmem((ROWS, W, B), f32),
-            pltpu.SMEM((3, ROWS, SLOTS), jnp.int32),
+            pltpu.SMEM((3, SLOTS, ROWS), jnp.int32),
             vmem((EMPTY + 1, W, B), bf),
             vmem((2, 2, 4, 4, CAP, W, B), bf),
             vmem((LEV * CAP, W, B), f32),
@@ -347,7 +343,7 @@
         compiler_params=pltpu.CompilerParams(
             collective_id=0, has_side_effects=True, vmem_limit_bytes=56 * 1024 * 1024
         ),
-    )(factor_blocks, pattern, levels, diag_inverse, right_side)
+    )(factor_blocks, pattern.T, levels, diag_inverse, jnp.swapaxes(right_side, 1, 2))
     return jnp.swapaxes(out, 1, 2)
 
 

time: 119 us -> 115 us (0.966)
  local copies, waits for them, and re-layouts: 5.31 us -> 1.67 us
    unnamed x3 -> x1, local copies, waits for them, and re-layouts: 5.31 us -> 1.67 us
where the time goes in v6:
time: 115 us
  Pallas kernels  113 us (98%)
  local copies, waits for them, and re-layouts  1.67 us (1%)
    pallas_call x1, Pallas kernels, per_device(): pl.pallas_call(kernel, out_shape=jax.ShapeDtypeStruct((ROWS, W, B), f32),...  113 us

profile of v6, /device:TPU:1, one launch (start us, length us, event | category | flops | bytes accessed | tf_op | source)
XLA Modules:
  0.0 115.1 jit_solution(3172544549911358456)
XLA Ops:
  0.0 113.4 %shard_map.55 = f32[16,32,128]{2,1,0:T(8,128)} custom-call(bf16[16,5,128,128]{3,2,1,0:T(8,128)(2,1)} %factor.1, s32[5,16]{1,0:T(8,128)} %bitcast.5, s32[512]{0:T(512)} %levels.1, f32[16,128,128]{2,1,0:T(8,128)} %inverse.1, f32[16,32,128]{2,1,0:T(8,128)} %bitcast.4), custom_call_target="tpu_custom_call" | custom-call | tf_op jit(solution)/shard_map/pallas_call | solution.py:313
  113.5 1.7 %copy.7 = f32[16,128,32]{1,2,0:T(8,128)} copy(f32[16,128,32]{1,2,0:T(8,128)} %bitcast.3) | data formatting | bytes 524288

commit v7 on v6

--- a/solution.py
+++ b/solution.py
@@ -63,8 +63,6 @@
         pltpu.make_async_copy(right.at[0:CAP], rhs.at[0:CAP], local_sem.at[3]),
         pltpu.make_async_copy(right.at[CAP:ROWS], rhs.at[CAP:ROWS], local_sem.at[4]),
     ]
-    for i in (2, 0, 3, 1, 4):
-        own[i].start()
 
     offsets = [(dx, dy) for dx in range(4) for dy in range(4) if (dx, dy) != (0, 0)]
     offsets.sort(key=lambda o: -(min(o[0], 4 - o[0]) + min(o[1], 4 - o[1])))
@@ -76,6 +74,8 @@
     greeted = [partner] + [along_z(by) for by in (1, 2, 3)] + [in_plane(*o) for o in offsets]
     for to in greeted:
         pl.semaphore_signal(barrier, inc=1, device_id=to, device_id_type=MESH)
+    for i in (2, 0, 3, 1, 4):
+        own[i].start()
     table[EMPTY] = jnp.zeros(table.shape[1:], table.dtype)
 
     def count_below(level):
@@ -192,6 +192,15 @@
     def from_late(t):
         return pltpu.make_async_copy(late.at[t - EARLY], blocks.at[t], late_sem.at[t - EARLY])
 
+    def give(some):
+        for r in some:
+            its = levels[row * ROWS + r]
+            rank = jnp.int32(0)
+            for back in (1, 2):
+                if r >= back:
+                    rank += (levels[row * ROWS + r - back] == its).astype(jnp.int32)
+            out[r] = sol[its * CAP + rank]
+
     def body(level, carry):
         p = lax.rem(level - 1, 2)
         p_next = lax.rem(level, 2)
@@ -207,6 +216,10 @@
 
         find(level)
 
+        @pl.when(level == LEV - 1)
+        def _():
+            give(range(ROWS - CAP))
+
         @pl.when((level >= 2) & (level <= 4))
         def _():
             pass_on(3 * level - 3)
@@ -226,9 +239,9 @@
             for t in range(1, EARLY):
                 pass_on(t)
             send_ahead(EARLY)
+            send_ahead(EARLY + 1)
             for t in range(EARLY):
                 arrive(t)
-            send_ahead(EARLY + 1)
             send_ahead(EARLY + 2)
 
         @pl.when((level >= 2) & (level <= 4))
@@ -298,13 +311,7 @@
     for t in range(SENT):
         for copy in direct(t) + [forward(t)]:
             copy.wait_send()
-    for r in range(ROWS):
-        its = levels[row * ROWS + r]
-        rank = jnp.int32(0)
-        for back in (1, 2):
-            if r >= back:
-                rank += (levels[row * ROWS + r - back] == its).astype(jnp.int32)
-        out[r] = sol[its * CAP + rank]
+    give(range(ROWS - CAP, ROWS))
 
 
 def per_device(factor_blocks, pattern, levels, diag_inverse, right_side):
@@ -312,7 +319,7 @@
     vmem = pltpu.VMEM
     out = pl.pallas_call(
         kernel,
-        out_shape=jax.ShapeDtypeStruct((ROWS, W, B), f32),
+        out_shape=pltpu.VMEM((ROWS, W, B), f32),
         in_specs=[
             pl.BlockSpec(memory_space=pl.ANY),
             pl.BlockSpec(memory_space=pltpu.SMEM),

time: 115 us -> 112 us (0.974)
  Pallas kernels: 113 us -> 111 us
    pallas_call x1, Pallas kernels: 113 us -> 111 us  [per_device(): pl.pallas_call(kernel, out_shape=pltpu.VMEM((ROWS, W, B), f32), in_specs=...]
where the time goes in v7:
time: 112 us
  Pallas kernels  111 us (99%)
    pallas_call x1, Pallas kernels, per_device(): pl.pallas_call(kernel, out_shape=pltpu.VMEM((ROWS, W, B), f32), in_specs=...  111 us

profile of v7, /device:TPU:1, one launch (start us, length us, event | category | flops | bytes accessed | tf_op | source)
XLA Modules:
  0.0 112.1 jit_solution(12974417273108500964)
XLA Ops:
  0.0 111.4 %shard_map.55 = f32[16,32,128]{2,1,0:T(8,128)S(1)} custom-call(bf16[16,5,128,128]{3,2,1,0:T(8,128)(2,1)} %factor.1, s32[5,16]{1,0:T(8,128)} %bitcast.5, s32[512]{0:T(512)} %levels.1, f32[16,128,128]{2,1,0:T(8,128)} %inverse.1, f32[16,32,128]{2,1,0:T(8,128)} %bitcast.4), custom_call_target="tpu_custom_call" | custom-call | tf_op jit(solution)/shard_map/pallas_call | solution.py:320
  111.4 0.7 copy.7

commit v8 on v7

--- a/solution.py
+++ b/solution.py
@@ -192,6 +192,10 @@
     def from_late(t):
         return pltpu.make_async_copy(late.at[t - EARLY], blocks.at[t], late_sem.at[t - EARLY])
 
+    def sent(p):
+        for o in offsets:
+            spread(p, *o).wait_send()
+
     def give(some):
         for r in some:
             its = levels[row * ROWS + r]
@@ -216,6 +220,10 @@
 
         find(level)
 
+        @pl.when(level >= 2)
+        def _():
+            sent(p_next)
+
         @pl.when(level == LEV - 1)
         def _():
             give(range(ROWS - CAP))
@@ -264,8 +272,6 @@
             arrive(level + 7)
             from_late(level + 7).start()
 
-        for o in offsets:
-            spread(p, *o).wait_send()
         for dx in range(4):
             across(p, dx, q).wait_send()
             across(p, dx, 1 - q).wait_recv()
@@ -277,7 +283,7 @@
                     table[(((level - 1) * 2 + core) * 16 + i) * CAP + c] = land[p, core, a, b, c]
             return carry
 
-        lax.fori_loop(0, 16, to_table, 0)
+        lax.fori_loop(0, 16, to_table, 0, unroll=4)
 
         @pl.when((level >= 2) & (level <= 4))
         def _():
@@ -291,9 +297,9 @@
         for c in range(CAP):
             r = rows[c]
             total = None
-            for k in range(0, 4 * SLOTS, 2):
-                pieces = [table[lookup[c * 4 * SLOTS + k + i]] for i in range(2)]
-                factors = [blocks[places[c], lax.rem(z + (k + i) // SLOTS, 4), (k + i) % SLOTS] for i in range(2)]
+            for k in range(0, 4 * SLOTS, 4):
+                pieces = [table[lookup[c * 4 * SLOTS + k + i]] for i in range(4)]
+                factors = [blocks[places[c], lax.rem(z + (k + i) // SLOTS, 4), (k + i) % SLOTS] for i in range(4)]
                 term = dot_t(jnp.concatenate(pieces, axis=1), jnp.concatenate(factors, axis=1))
                 total = term if total is None else total + term
             v = times_inverse(rhs[r] - total, inv_terms[r])
@@ -307,6 +313,7 @@
         return carry
 
     lax.fori_loop(1, LEV, body, 0)
+    sent((LEV - 2) % 2)
 
     for t in range(SENT):
         for copy in direct(t) + [forward(t)]:

time: 112 us -> 112 us (level)
  no operation moved by 1% of the time
where the time goes in v8:
time: 112 us
  Pallas kernels  111 us (99%)
    pallas_call x1, Pallas kernels, per_device(): pl.pallas_call(kernel, out_shape=pltpu.VMEM((ROWS, W, B), f32), in_specs=...  111 us

profile of v8, /device:TPU:1, one launch (start us, length us, event | category | flops | bytes accessed | tf_op | source)
XLA Modules:
  0.0 111.8 jit_solution(4328353596445427085)
XLA Ops:
  0.0 111.1 %shard_map.55 = f32[16,32,128]{2,1,0:T(8,128)S(1)} custom-call(bf16[16,5,128,128]{3,2,1,0:T(8,128)(2,1)} %factor.1, s32[5,16]{1,0:T(8,128)} %bitcast.5, s32[512]{0:T(512)} %levels.1, f32[16,128,128]{2,1,0:T(8,128)} %inverse.1, f32[16,32,128]{2,1,0:T(8,128)} %bitcast.4), custom_call_target="tpu_custom_call" | custom-call | tf_op jit(solution)/shard_map/pallas_call | solution.py:327
  111.1 0.7 copy.7

commit v9 on v8

--- a/solution.py
+++ b/solution.py
@@ -140,11 +140,11 @@
 
     def spread(p, dx, dy):
         unit = land.at[p, q, x, y]
-        return remote(unit, unit, gs.at[p, dx, dy], gr.at[p, dx, dy], in_plane(dx, dy))
-
-    def spread_in(p, dx, dy):
-        unit = land.at[p, q, lax.rem(x + 4 - dx, 4), lax.rem(y + 4 - dy, 4)]
-        return remote(unit, unit, gs.at[p, dx, dy], gr.at[p, dx, dy], in_plane(dx, dy))
+        return remote(unit, unit, gs.at[p, dx], gr.at[p, dx], in_plane(dx, dy))
+
+    def spread_group(p, dx):
+        unit = land.at[p, q, lax.rem(x + 4 - dx, 4), pl.ds(0, 4 if dx else 3)]
+        return remote(unit, unit, gs.at[p, dx], gr.at[p, dx], partner)
 
     def across(p, dx, core):
         unit = land.at[p, core, lax.rem(x + 4 - dx, 4)]
@@ -193,8 +193,8 @@
         return pltpu.make_async_copy(late.at[t - EARLY], blocks.at[t], late_sem.at[t - EARLY])
 
     def sent(p):
-        for o in offsets:
-            spread(p, *o).wait_send()
+        for dx in range(4):
+            spread_group(p, dx).wait_send()
 
     def give(some):
         for r in some:
@@ -237,9 +237,7 @@
             pass_on(2 * level + 2)
 
         for dx in (0, 1, 3, 2):
-            for dy in (1, 3, 2, 0):
-                if (dx, dy) != (0, 0):
-                    spread_in(p, dx, dy).wait_recv()
+            spread_group(p, dx).wait_recv()
             across(p, dx, q).start()
 
         @pl.when(level == 1)
@@ -273,7 +271,6 @@
             from_late(level + 7).start()
 
         for dx in range(4):
-            across(p, dx, q).wait_send()
             across(p, dx, 1 - q).wait_recv()
 
         def to_table(i, carry):
@@ -297,14 +294,17 @@
         for c in range(CAP):
             r = rows[c]
             total = None
-            for k in range(0, 4 * SLOTS, 4):
-                pieces = [table[lookup[c * 4 * SLOTS + k + i]] for i in range(4)]
-                factors = [blocks[places[c], lax.rem(z + (k + i) // SLOTS, 4), (k + i) % SLOTS] for i in range(4)]
+            for k in range(0, 4 * SLOTS, 20):
+                pieces = [table[lookup[c * 4 * SLOTS + k + i]] for i in range(20)]
+                factors = [blocks[places[c], lax.rem(z + (k + i) // SLOTS, 4), (k + i) % SLOTS] for i in range(20)]
                 term = dot_t(jnp.concatenate(pieces, axis=1), jnp.concatenate(factors, axis=1))
                 total = term if total is None else total + term
             v = times_inverse(rhs[r] - total, inv_terms[r])
             sol[level * CAP + c] = v
             land[p_next, q, x, y, c] = v.astype(jnp.bfloat16)
+
+        for dx in range(4):
+            across(p, dx, q).wait_send()
 
         @pl.when(level < LEV - 1)
         def _():
@@ -352,7 +352,7 @@
             pltpu.SMEM((CAP,), jnp.int32),
             dma((5,)), dma((SENT - EARLY,)), dma((3,)), dma((3,)),
             dma((SENT, 3)), dma((SENT, 3)),
-            dma((2, 4, 4)), dma((2, 4, 4)), dma((2, 4)), dma((2, 4)),
+            dma((2, 4)), dma((2, 4)), dma((2, 4)), dma((2, 4)),
         ],
         compiler_params=pltpu.CompilerParams(
             collective_id=0, has_side_effects=True, vmem_limit_bytes=56 * 1024 * 1024

time: 112 us -> 111 us (level)
    pallas_call x1, Pallas kernels: 111 us -> 110 us  [per_device(): pl.pallas_call(kernel, out_shape=pltpu.VMEM((ROWS, W, B), f32), in_specs=...]
where the time goes in v9:
time: 111 us
  Pallas kernels  110 us (99%)
    pallas_call x1, Pallas kernels, per_device(): pl.pallas_call(kernel, out_shape=pltpu.VMEM((ROWS, W, B), f32), in_specs=...  110 us

profile of v9, /device:TPU:1, one launch (start us, length us, event | category | flops | bytes accessed | tf_op | source)
XLA Modules:
  0.0 110.6 jit_solution(14372042256810568987)
XLA Ops:
  0.0 109.9 %shard_map.55 = f32[16,32,128]{2,1,0:T(8,128)S(1)} custom-call(bf16[16,5,128,128]{3,2,1,0:T(8,128)(2,1)} %factor.1, s32[5,16]{1,0:T(8,128)} %bitcast.5, s32[512]{0:T(512)} %levels.1, f32[16,128,128]{2,1,0:T(8,128)} %inverse.1, f32[16,32,128]{2,1,0:T(8,128)} %bitcast.4), custom_call_target="tpu_custom_call" | custom-call | tf_op jit(solution)/shard_map/pallas_call | solution.py:327
  109.9 0.7 copy.7

commit v10 on v9

--- a/solution.py
+++ b/solution.py
@@ -227,6 +227,9 @@
         @pl.when(level == LEV - 1)
         def _():
             give(range(ROWS - CAP))
+            for t in range(SENT):
+                for copy in direct(t) + [forward(t)]:
+                    copy.wait_send()
 
         @pl.when((level >= 2) & (level <= 4))
         def _():
@@ -315,9 +318,6 @@
     lax.fori_loop(1, LEV, body, 0)
     sent((LEV - 2) % 2)
 
-    for t in range(SENT):
-        for copy in direct(t) + [forward(t)]:
-            copy.wait_send()
     give(range(ROWS - CAP, ROWS))
 
 

time: 111 us -> 111 us (level)
  no operation moved by 1% of the time
where the time goes in v10:
time: 111 us
  Pallas kernels  110 us (99%)
    pallas_call x1, Pallas kernels, per_device(): pl.pallas_call(kernel, out_shape=pltpu.VMEM((ROWS, W, B), f32), in_specs=...  110 us

profile of v10, /device:TPU:1, one launch (start us, length us, event | category | flops | bytes accessed | tf_op | source)
XLA Modules:
  0.0 110.5 jit_solution(8241664089753440797)
XLA Ops:
  0.0 109.8 %shard_map.55 = f32[16,32,128]{2,1,0:T(8,128)S(1)} custom-call(bf16[16,5,128,128]{3,2,1,0:T(8,128)(2,1)} %factor.1, s32[5,16]{1,0:T(8,128)} %bitcast.5, s32[512]{0:T(512)} %levels.1, f32[16,128,128]{2,1,0:T(8,128)} %inverse.1, f32[16,32,128]{2,1,0:T(8,128)} %bitcast.4), custom_call_target="tpu_custom_call" | custom-call | tf_op jit(solution)/shard_map/pallas_call | solution.py:327
  109.8 0.7 copy.7

commit v11 on v9

--- a/solution.py
+++ b/solution.py
@@ -236,7 +236,7 @@
         def _():
             pass_on(2 * level + 2)
 
-        for dx in (0, 1, 3, 2):
+        for dx in (1, 3, 0, 2):
             spread_group(p, dx).wait_recv()
             across(p, dx, q).start()
 

time: 111 us -> 111 us (level)
  no operation moved by 1% of the time
where the time goes in v11:
time: 111 us; the launch traced here: 110 us
  Pallas kernels  110 us (99%)
    pallas_call x1, Pallas kernels, per_device(): pl.pallas_call(kernel, out_shape=pltpu.VMEM((ROWS, W, B), f32), in_specs=...  110 us

profile of v11, /device:TPU:1, one launch (start us, length us, event | category | flops | bytes accessed | tf_op | source)
XLA Modules:
  0.0 110.5 jit_solution(8585980969878244467)
XLA Ops:
  0.0 109.7 %shard_map.55 = f32[16,32,128]{2,1,0:T(8,128)S(1)} custom-call(bf16[16,5,128,128]{3,2,1,0:T(8,128)(2,1)} %factor.1, s32[5,16]{1,0:T(8,128)} %bitcast.5, s32[512]{0:T(512)} %levels.1, f32[16,128,128]{2,1,0:T(8,128)} %inverse.1, f32[16,32,128]{2,1,0:T(8,128)} %bitcast.4), custom_call_target="tpu_custom_call" | custom-call | tf_op jit(solution)/shard_map/pallas_call | solution.py:327
  109.8 0.7 copy.7
